TPU v7x, 32 devices: a whole 2x2x4 slice. The times are simulated.
32 devices in a mesh: seq: 8 (over y, x, core), head: 4 (over z).
Axes of the slice: x: 2, y: 2, z: 4, core: 2. Of those that a mesh axis runs over, the one named last changes fastest.
Arguments:
- queries: bfloat16 [32, 2048, 128], P('head', 'seq'), may hold values from -0.5390625 to 0.5390625
- keys: bfloat16 [32, 2048, 128], P('head', 'seq'), may hold values from -0.5390625 to 0.5390625
- values: bfloat16 [32, 2048, 128], P('head', 'seq'), may hold values from -15 to 15
- log_decay: float32 [32, 2048], P('head', 'seq'), may hold values from -1 to 0, as said below
- level_weight: float32 [32, 21, 2048], P('head', None, 'seq'), may hold values from 0.2 to 2
- gate_input: bfloat16 [32, 2048, 128], P('head', 'seq'), may hold values from -6 to 6
- norm_gain: float32 [32, 128], P('head'), may hold values from 0.5 to 1.5
- out_grad: bfloat16 [32, 2048, 128], P('head', 'seq'), may hold values from -15 to 15
Outputs:
- layer_out: bfloat16 [32, 2048, 128], P('head', 'seq')
- grad_queries: bfloat16 [32, 2048, 128], P('head', 'seq')
- grad_keys: bfloat16 [32, 2048, 128], P('head', 'seq')
- grad_values: bfloat16 [32, 2048, 128], P('head', 'seq')
- grad_levels: float32 [32, 21, 2048], P('head', None, 'seq')
- grad_gate: bfloat16 [32, 2048, 128], P('head', 'seq')
- grad_gain: float32 [32, 128], P('head')
Inputs may be any that keep to these rules, and one draw needn't show every extreme that they name: `log_decay`: negative logarithms of decays.
All inputs are finite; a program needn't handle non-finite values.
Results may differ from a plain program's by a relative error of at most 0.0051.
Values sent between devices are 32-bit elements; how exact they have to be, the bound alone decides.
A program may use at most 64 MiB of HBM per device.

v0:
```python
import jax
import jax.numpy as jnp
from jax import lax
from jax.sharding import PartitionSpec as P

HEADS = 32
HEAD_DIM = 128


EPSILON = 1e-05
HIGH = lax.Precision.HIGHEST


def partner(block, axis, distance):
    count = lax.axis_size(axis)
    route = []
    for low in range(count):
        high = low | 1 << distance
        if high != low and high < count:
            route += [(low, high), (high, low)]
    return lax.ppermute(block, axis, route)


def level_table(row_start, rows, width, depth):
    row_ids = row_start + lax.iota(jnp.int32, rows)
    column_ids = lax.iota(jnp.int32, width)
    crossed = jnp.bitwise_xor(row_ids[:, None], column_ids[None, :])
    level = jnp.zeros((rows, width), jnp.int32)
    for shift in range(depth):
        level = level + (jnp.right_shift(crossed, shift) > 0).astype(jnp.int32)
    causal = column_ids[None, :] <= row_ids[:, None]
    return (level, causal)


def pair_weights(running, mix_rows, row_start, rows, depth):
    level, causal = level_table(row_start, rows, running.shape[1], depth)
    spread = jnp.where(causal[None], running[:, :, None] - running[:, None, :], 0.0)
    decay = jnp.where(causal[None], jnp.exp(spread), 0.0)
    chosen = jnp.zeros_like(decay)
    for place in range(depth + 1):
        chosen = chosen + jnp.where((level == place)[None], mix_rows[:, place, :, None], 0.0)
    return (decay, chosen, level)


def intra_forward(queries, keys, values, running, mix, depth):
    heads, width, state = queries.shape
    rows = min(width, 512)

    def one_block(index):
        start = index * rows
        decay, chosen, level = pair_weights(running, mix, start, rows, depth)
        scores = jnp.einsum("hik,hjk->hij", queries, keys, preferred_element_type=jnp.float32)
        mixing = (scores * decay * chosen).astype(jnp.bfloat16)
        return jnp.einsum("hij,hjp->hip", mixing, values, preferred_element_type=jnp.float32)

    blocks = lax.map(one_block, jnp.arange(width // rows, dtype=jnp.int32))
    return jnp.moveaxis(blocks, 0, 1).reshape(heads, width, -1)


def intra_backward(queries, keys, values, running, mix, grad_mixed, depth):
    heads, width, state = queries.shape
    rows = min(width, 512)

    def one_block(carry, index):
        grad_keys, grad_values = carry
        start = index * rows
        decay, chosen, level = pair_weights(running, mix, start, rows, depth)
        scores = jnp.einsum("hik,hjk->hij", queries, keys, preferred_element_type=jnp.float32)
        weight = decay * chosen
        mixing = (scores * weight).astype(jnp.bfloat16)
        grad_mixing = jnp.einsum(
            "hip,hjp->hij", grad_mixed, values, preferred_element_type=jnp.float32
        )
        grad_scores = (grad_mixing * weight).astype(jnp.bfloat16)
        grad_q_rows = jnp.einsum(
            "hij,hjk->hik", grad_scores, keys, preferred_element_type=jnp.float32
        )
        grad_keys = grad_keys + jnp.einsum(
            "hij,hik->hjk", grad_scores, queries, preferred_element_type=jnp.float32
        )
        grad_values = grad_values + jnp.einsum(
            "hij,hip->hjp", mixing, grad_mixed, preferred_element_type=jnp.float32
        )
        moved = grad_mixing * scores * decay
        per_level = jnp.stack(
            [
                jnp.sum(jnp.where((level == place)[None], moved, 0.0), axis=2)
                for place in range(depth + 1)
            ],
            axis=1,
        )
        return ((grad_keys, grad_values), (grad_q_rows, per_level))

    start_carry = (
        jnp.zeros((heads, width, state), jnp.float32),
        jnp.zeros((heads, width, values.shape[2]), jnp.float32),
    )
    (grad_keys, grad_values), (q_blocks, level_blocks) = lax.scan(
        one_block, start_carry, jnp.arange(width // rows, dtype=jnp.int32)
    )
    grad_queries = jnp.moveaxis(q_blocks, 0, 1).reshape(heads, width, state)
    grad_levels = jnp.moveaxis(level_blocks, 0, 2).reshape(heads, depth + 1, width)
    return (grad_queries, grad_keys, grad_values, grad_levels)


def local(queries, keys, values, log_decay, level_weight, gate_input, norm_gain, out_grad):
    heads, width, state = queries.shape
    depth = width.bit_length() - 1
    count = lax.axis_size("seq")
    levels_dev = count.bit_length() - 1
    current = lax.axis_index("seq")
    running = jnp.cumsum(log_decay, axis=1)
    intra_mix = level_weight[:, : depth + 1, :]
    inter_mix = level_weight[:, depth + 1 : depth + 1 + levels_dev, :]
    inner = intra_forward(queries, keys, values, running, intra_mix, depth)
    tail = jnp.exp(running[:, -1:] - running)
    keys_wide = keys.astype(jnp.float32)
    values_wide = values.astype(jnp.float32)
    queries_wide = queries.astype(jnp.float32)
    own_state = jnp.einsum(
        "hjk,hjp->hkp", keys_wide * tail[:, :, None], values_wide, precision=HIGH
    )
    stretch_total = running[:, -1]
    group_sum = own_state
    group_rate = stretch_total
    ahead = jnp.zeros((heads,), jnp.float32)
    stored = []
    factors = []
    for bit in range(levels_dev):
        other_sum, other_rate = partner((group_sum, group_rate), "seq", bit)
        upper = jnp.bitwise_and(jnp.right_shift(current, bit), 1) == 1
        taken = jnp.where(upper, jnp.exp(ahead), 0.0)
        own_factor = jnp.where(upper, 1.0, jnp.exp(other_rate))
        other_factor = jnp.where(upper, jnp.exp(group_rate), 1.0)
        stored.append(taken[:, None, None] * other_sum)
        factors.append((own_factor, other_factor, taken))
        group_sum = own_factor[:, None, None] * group_sum + other_factor[:, None, None] * other_sum
        ahead = ahead + jnp.where(upper, other_rate, 0.0)
        group_rate = group_rate + other_rate
    buckets = jnp.stack(stored, axis=0)
    reach = inter_mix * jnp.exp(running)[:, None, :]
    through_q = jnp.einsum("hik,lhkp->lhip", queries_wide, buckets, precision=HIGH)
    outer = jnp.einsum("hli,lhip->hip", reach, through_q, precision=HIGH)
    mixed = inner + outer
    gate = gate_input.astype(jnp.float32)
    sigmoid_gate = jax.nn.sigmoid(gate)
    gate_act = gate * sigmoid_gate
    gated = mixed * gate_act
    grad_y = out_grad.astype(jnp.float32)
    gain = norm_gain[:, None, :]
    scaled = grad_y * gain
    square_sum, cross = lax.psum(
        (jnp.sum(gated * gated, axis=(0, 2)), jnp.sum(gated * scaled, axis=(0, 2))), "head"
    )
    total = HEADS * HEAD_DIM
    inverse = lax.rsqrt(square_sum / total + EPSILON)[None, :, None]
    layer_out = (gain * gated * inverse).astype(jnp.bfloat16)
    grad_gated = inverse * scaled - gated * (
        inverse * inverse * inverse * cross[None, :, None] / total
    )
    grad_gain = lax.psum(jnp.sum(grad_y * gated * inverse, axis=1), "seq")
    grad_gate = (grad_gated * mixed * sigmoid_gate * (1.0 + gate * (1.0 - sigmoid_gate))).astype(
        jnp.bfloat16
    )
    grad_mixed = (grad_gated * gate_act).astype(jnp.bfloat16)
    gq_in, gk_in, gv_in, glev_in = intra_backward(
        queries, keys, values, running, intra_mix, grad_mixed, depth
    )
    grad_wide = grad_mixed.astype(jnp.float32)
    glev_out = jnp.exp(running)[:, None, :] * jnp.einsum(
        "lhip,hip->hli", through_q, grad_wide, precision=HIGH
    )
    scaled_q = reach[:, :, :, None] * queries_wide[:, None]
    bucket_grads = jnp.einsum("hlik,hip->lhkp", scaled_q, grad_wide, precision=HIGH)
    pulled = jnp.einsum("lhkp,hip->lhik", buckets, grad_wide, precision=HIGH)
    gq_out = jnp.einsum("hli,lhik->hik", reach, pulled, precision=HIGH)
    downward = jnp.zeros_like(own_state)
    for bit in reversed(range(levels_dev)):
        own_factor, other_factor, taken = factors[bit]
        message = other_factor[:, None, None] * downward + taken[:, None, None] * bucket_grads[bit]
        received = partner(message, "seq", bit)
        downward = own_factor[:, None, None] * downward + received
    gk_out = tail[:, :, None] * jnp.einsum("hkp,hjp->hjk", downward, values_wide, precision=HIGH)
    gv_out = tail[:, :, None] * jnp.einsum("hkp,hjk->hjp", downward, keys_wide, precision=HIGH)
    rest = level_weight.shape[1] - depth - 1 - levels_dev
    grad_levels = jnp.concatenate(
        [glev_in, glev_out, jnp.zeros((heads, rest, width), jnp.float32)], axis=1
    )
    grad_queries = (gq_in + gq_out).astype(jnp.bfloat16)
    grad_keys = (gk_in + gk_out).astype(jnp.bfloat16)
    grad_values = (gv_in + gv_out).astype(jnp.bfloat16)
    return (layer_out, grad_queries, grad_keys, grad_values, grad_levels, grad_gate, grad_gain)


def solution(mesh):
    in_specs = (
        P("head", "seq", None),
        P("head", "seq", None),
        P("head", "seq", None),
        P("head", "seq"),
        P("head", None, "seq"),
        P("head", "seq", None),
        P("head", None),
        P("head", "seq", None),
    )
    out_specs = (
        P("head", "seq", None),
        P("head", "seq", None),
        P("head", "seq", None),
        P("head", "seq", None),
        P("head", None, "seq"),
        P("head", "seq", None),
        P("head", None),
    )
    return jax.shard_map(local, mesh=mesh, in_specs=in_specs, out_specs=out_specs, check_vma=False)
```

profile of v0, /device:TPU:0, one launch (start us, length us, event | category | flops | bytes accessed | tf_op | source)
XLA Modules:
  0.0 173.6 jit_solution(11691833936328463032)
XLA Ops:
  3.7 2.4 %fusion.33 = f32[8,128,128]{2,1,0:T(8,128)S(1)} fusion(bf16[8,256,128]{2,1,0:T(8,128)(2,1)S(1)} %copy-done, bf16[8,256,128]{2,1,0:T(8,128)(2,1)} %param.9, f32[8,256]{1,0:T(8,128)S(1)} %subtract_exponential_fusion), kind=kOutput, calls=%fused_computation.63 | convolution fusion | flops 403177472 | bytes 1581056 | tf_op jit(solution)/shard_map/hjk,hjp->hkp/dot_general | solution.py:120
  14.7 3.0 %collective-permute-start.3 = (f32[8]{0:T(128)S(1)}, f32[8]{0:T(128)S(1)}, u32[]{:S(2)}, u32[]{:S(2)}) collective-permute-start(f32[8]{0:T(128)S(1)} %get-tuple-element.104), channel_id=1, source_target_pairs={{0,8},{8,0},{4,12},{12,4},{16,24},{24,16},{20,28},{28,20},{1,9},{9... | collective-permute-start | bytes 104 | tf_op jit(solution)/shard_map/ppermute | solution.py:21
  20.4 2.0 %collective-permute-start.2 = (f32[8,128,128]{2,1,0:T(8,128)S(1)}, f32[8,128,128]{2,1,0:T(8,128)S(1)}, u32[]{:S(2)}, u32[]{:S(2)}) collective-permute-start(f32[8,128,128]{2,1,0:T(8,128)S(1)} %get-tuple-element.108), channel_id=1, source_target_pairs={{0,8},{8,0},{4,12},{12,4},{16,24},{24,16},{20,28},{28,20},{1,9},{9... | collective-permute-start | bytes 1572872 | tf_op jit(solution)/shard_map/ppermute | solution.py:21
  24.4 8.9 %collective-permute-done.2 = f32[8,128,128]{2,1,0:T(8,128)S(1)} collective-permute-done((f32[8,128,128]{2,1,0:T(8,128)S(1)}, f32[8,128,128]{2,1,0:T(8,128)S(1)}, u32[]{:S(2)}, u32[]{:S(2)}) %collective-permute-start.2) | collective-permute-done | bytes 524320 | tf_op jit(solution)/shard_map/ppermute | solution.py:21
  33.6 1.8 %collective-permute-start.4 = (f32[8,128,128]{2,1,0:T(8,128)S(1)}, f32[8,128,128]{2,1,0:T(8,128)S(1)}, u32[]{:S(2)}, u32[]{:S(2)}) collective-permute-start(f32[8,128,128]{2,1,0:T(8,128)S(1)} %get-tuple-element.110), channel_id=1, source_target_pairs={{0,16},{16,0},{4,20},{20,4},{8,24},{24,8},{12,28},{28,12},{1,17},{... | collective-permute-start | bytes 1572872 | tf_op jit(solution)/shard_map/ppermute | solution.py:21
  36.1 9.6 %collective-permute-done.5 = f32[8]{0:T(128)S(1)} collective-permute-done((f32[8]{0:T(128)S(1)}, f32[8]{0:T(128)S(1)}, u32[]{:S(2)}, u32[]{:S(2)}) %collective-permute-start.5) | collective-permute-done | bytes 64 | tf_op jit(solution)/shard_map/ppermute | solution.py:21
  46.5 3.4 %fusion.3 = (f32[8,256,128]{1,2,0:T(8,128)S(1)}, f32[8,3,128,256]{3,2,1,0:T(8,128)}) fusion(f32[8,256,3]{1,2,0:T(4,128)S(1)} %copy-done.36, bf16[8,256,128]{2,1,0:T(8,128)(2,1)S(1)} %copy-done.1, f32[1,8,128,128]{3,2,1,0:T(8,128)S(1)} %multiply_bitcast_fusion, f32[1,8,128,128]{3,2,1,0:T(8,128)S(1)} %get-tuple-element.109, ...), kind=kOutput, calls=%fused_computation.5 | convolution fusion | flops 1210056704 | bytes 6316032 | tf_op jit(solution)/shard_map/hik,lhkp->lhip/dot_general | solution.py:142
  50.0 5.0 %multiply_reduce_fusion = (f32[256]{0:T(256)}, f32[8,256,128]{1,2,0:T(8,128)}, f32[8,256,128]{1,2,0:T(8,128)}) fusion(bf16[8,256,128]{1,2,0:T(8,128)(2,1)S(1)} %copy-done.17, f32[8,256,128]{1,2,0:T(8,128)S(1)} %get-tuple-element.125, bf16[8,256,128]{2,1,0:T(8,128)(2,1)S(1)} %copy-done, f32[8,256,256]{1,2,0:T(8,128)S(1)} %fusion.66, ...), kind=kOutput, calls=%fused_computation.62 | convolution fusion | flops 148635392 | bytes 7029760 | tf_op jit(solution)/shard_map/while/body/eval_jaxpr/hij,hjp->hip/dot_general | solution.py:54
  55.0 12.6 %psum.21 = f32[256]{0:T(256)} all-reduce(f32[256]{0:T(256)} %get-tuple-element.99), channel_id=1, replica_groups=mesh['seq'=8,'head'=4] {'head'}, use_global_device_ids=true, to_apply=%region_3.4 | all-reduce | flops 256 | bytes 2048 | tf_op jit(solution)/shard_map/psum | solution.py:152
  68.8 2.4 %fusion.25 = (f32[8,128]{1,0:T(8,128)}, f32[256]{0:T(256)}) fusion(f32[8,256,128]{1,2,0:T(8,128)} %get-tuple-element.100, bf16[8,256,128]{1,2,0:T(8,128)(2,1)} %copy.58, f32[256]{0:T(256)S(1)} %add_rsqrt_fusion, f32[8,128]{1,0:T(8,128)} %param.14), kind=kLoop, calls=%fused_computation.52 | loop fusion | flops 1833728 | bytes 1583104 | tf_op jit(solution)/shard_map/reduce_sum | solution.py:161
  71.3 9.2 %psum.22 = f32[256]{0:T(256)} all-reduce(f32[256]{0:T(256)} %get-tuple-element.92), channel_id=1, replica_groups=mesh['seq'=8,'head'=4] {'head'}, use_global_device_ids=true, to_apply=%region_5.6 | all-reduce | flops 256 | bytes 2048 | tf_op jit(solution)/shard_map/psum | solution.py:152
  81.3 4.1 %fusion.63 = (f32[8,256,128]{1,2,0:T(8,128)}, bf16[8,256,128]{1,2,0:T(8,128)(2,1)S(1)}, bf16[8,256,128]{1,2,0:T(8,128)(2,1)}, bf16[8,256,128]{1,2,0:T(8,128)(2,1)}) fusion(bf16[8,256,128]{1,2,0:T(8,128)(2,1)} %copy.57, f32[8,256,128]{1,2,0:T(8,128)} %get-tuple-element.100, f32[256]{0:T(256)S(1)} %fusion.56, f32[8,128]{1,0:T(8,128)} %param.14, ...), kind=kLoop, calls=%fused_computation.161 | loop fusion | flops 6029312 | bytes 5773312
  85.5 3.5 %multiply_convert_fusion.1 = (bf16[8,256,256]{1,2,0:T(8,128)(2,1)}, f32[8,256,256]{1,2,0:T(8,128)S(1)}) fusion(f32[8,256]{1,0:T(8,128)S(1)} %get-tuple-element.102, pred[256,256]{0,1:T(8,128)(4,1)S(1)} %get-tuple-element.130, f32[8,256]{1,0:T(8,128)S(1)} %copy-done.63, pred[256,256]{0,1:T(8,128)(4,1)S(1)} %get-tuple-element.131, ...), kind=kOutput, calls=%fused_computation.19 | convolution fusion | flops 146276352 | bytes 4931584 | tf_op jit(solution)/shard_map/while/body/eval_jaxpr/hip,hjp->hij/dot_general | solution.py:71
  89.0 3.2 %convolution_bitcast_fusion = f32[3,8,256,128]{3,2,0,1:T(8,128)} fusion(bf16[8,256,128]{1,2,0:T(8,128)(2,1)S(1)} %get-tuple-element.94, f32[1,8,128,128]{3,2,1,0:T(8,128)S(1)} %copy-done.13, f32[1,8,128,128]{3,2,1,0:T(8,128)S(1)} %copy-done.11, f32[1,8,128,128]{3,2,1,0:T(8,128)S(1)} %copy-done.9), kind=kOutput, calls=%fused_computation.24 | convolution fusion | flops 1208745984 | bytes 5242880 | tf_op jit(solution)/shard_map/lhkp,hip->lhik/dot_general | solution.py:175
  92.2 4.0 %select_reduce_fusion = (f32[8,256]{1,0:T(8,128)}, f32[8,256]{1,0:T(8,128)}, f32[8,256]{1,0:T(8,128)}, f32[8,256]{1,0:T(8,128)}, f32[8,256]{1,0:T(8,128)}, /*ind...) fusion(pred[256,256]{0,1:T(8,128)(4,1)S(1)} %get-tuple-element.131, ...), kind=kLoop, calls=%fused_computation.8 | loop fusion | flops 12040192 | bytes 4931584 | tf_op jit(solution)/shard_map/while/body/eval_jaxpr/reduce_sum | solution.py:87
  96.8 4.3 %fusion.7 = f32[3,8,128,128]{3,2,1,0:T(8,128)S(1)} fusion(bf16[8,256,128]{1,2,0:T(8,128)(2,1)S(1)} %get-tuple-element.94, f32[8,256,128]{2,1,0:T(8,128)S(1)} %copy-done.14, f32[8,3,256]{2,1,0:T(4,128)S(1)} %copy-done.35), kind=kOutput, calls=%fused_computation.30 | convolution fusion | flops 1208745984 | bytes 3170304 | tf_op jit(solution)/shard_map/hlik,hip->lhkp/dot_general | solution.py:174
  104.7 2.0 %copy.69 = bf16[8,256,128]{2,1,0:T(8,128)(2,1)} copy(bf16[8,256,128]{1,2,0:T(8,128)(2,1)} %get-tuple-element.106) | data formatting | bytes 1048576
  106.7 2.0 %copy.70 = bf16[8,256,128]{2,1,0:T(8,128)(2,1)} copy(bf16[8,256,128]{1,2,0:T(8,128)(2,1)} %get-tuple-element.105) | data formatting | bytes 1048576
  108.7 12.8 %psum.23 = f32[8,128]{1,0:T(8,128)} all-reduce(f32[8,128]{1,0:T(8,128)} %get-tuple-element.91), channel_id=1, replica_groups=mesh['seq'=8,'head'=4] {'seq'}, use_global_device_ids=true, to_apply=%region_16.17 | all-reduce | flops 1024 | bytes 8192 | tf_op jit(solution)/shard_map/psum | solution.py:161
  131.9 2.7 %fusion.2 = f32[8,256,3]{1,2,0:T(4,128)S(1)} fusion(f32[8,3,128,256]{3,2,1,0:T(8,128)} %get-tuple-element.126, f32[8,256,128]{1,2,0:T(8,128)} %get-tuple-element.93), kind=kLoop, calls=%fused_computation.3 | loop fusion | flops 1566720 | bytes 4218880
  135.9 15.4 %fusion = f32[8,256,1,128]{3,2,1,0:T(1,128)S(1)} fusion(f32[8,3,256,1]{1,3,2,0:T(1,128)S(1)} %copy-done.18, f32[3,8,256,128]{3,2,0,1:T(8,128)S(1)} %copy-done.16), kind=kOutput, calls=%fused_computation | convolution fusion | flops 9437184 | bytes 4218880 | tf_op jit(solution)/shard_map/hli,lhik->hik/dot_general | solution.py:176
  154.6 11.7 %collective-permute-done.7 = f32[8,128,128]{2,1,0:T(8,128)S(1)} collective-permute-done((f32[8,128,128]{2,1,0:T(8,128)S(1)}, f32[8,128,128]{2,1,0:T(8,128)S(1)}, u32[]{:S(2)}, u32[]{:S(2)}) %collective-permute-start.7) | collective-permute-done | bytes 524320 | tf_op jit(solution)/shard_map/ppermute | solution.py:21
  167.8 2.6 %fusion.32 = f32[8,256,128]{2,1,0:T(8,128)S(1)} fusion(bf16[8,256,128]{1,2,0:T(8,128)(2,1)S(1)} %copy-done.7, f32[8,256,256]{1,2,0:T(8,128)S(1)} %fusion.66, f32[8,256]{1,0:T(8,128)S(1)} %get-tuple-element.102, pred[256,256]{0,1:T(8,128)(4,1)S(1)} %get-tuple-element.130, f32[8,256]{1,0:T(8,128)S(1)} %copy-done.64, f32[8,256]{1,0:T(8,128)S(1)} %copy-done.43, ...), kind=kOutput, calls=%fused_computation.59 | convolution fusion | flops 146276352 | bytes 4407296 | tf_op jit(solution)/shard_map/while/body/eval_jaxpr/hij,hip->hjp/dot_general | solution.py:81
  170.4 1.6 fusion.19
  (218 shorter events, 41.8 us)
Async XLA Ops:
  2.5 12.2 %collective-permute-start.1 = (f32[8]{0:T(128)S(1)}, f32[8]{0:T(128)S(1)}, u32[]{:S(2)}, u32[]{:S(2)}) collective-permute-start(f32[8]{0:T(128)S(1)} %slice_reduce_fusion.1), channel_id=1, source_target_pairs={{0,4},{4,0},{8,12},{12,8},{16,20},{20,16},{24,28},{28,24},{1,5},{5... | collective-permute-start | bytes 104 | tf_op jit(solution)/shard_map/ppermute | solution.py:21
  6.1 13.8 %collective-permute-start = (f32[8,128,128]{2,1,0:T(8,128)S(1)}, f32[8,128,128]{2,1,0:T(8,128)S(1)}, u32[]{:S(2)}, u32[]{:S(2)}) collective-permute-start(f32[8,128,128]{2,1,0:T(8,128)S(1)} %fusion.33), channel_id=1, source_target_pairs={{0,4},{4,0},{8,12},{12,8},{16,20},{20,16},{24,28},{28,24},{1,5},{5... | collective-permute-start | bytes 1572872 | tf_op jit(solution)/shard_map/ppermute | solution.py:21
  14.7 4.5 %collective-permute-start.3 = (f32[8]{0:T(128)S(1)}, f32[8]{0:T(128)S(1)}, u32[]{:S(2)}, u32[]{:S(2)}) collective-permute-start(f32[8]{0:T(128)S(1)} %get-tuple-element.104), channel_id=1, source_target_pairs={{0,8},{8,0},{4,12},{12,4},{16,24},{24,16},{20,28},{28,20},{1,9},{9... | collective-permute-start | bytes 104 | tf_op jit(solution)/shard_map/ppermute | solution.py:21
  19.8 26.5 %copy-start.71 = (f32[8]{0:T(128)}, f32[8]{0:T(128)S(1)}, u32[]{:S(2)}) copy-start(f32[8]{0:T(128)S(1)} %get-tuple-element.121) | copy-start | bytes 100
  20.0 26.4 %copy-start.8 = (f32[1,8,128,128]{3,2,1,0:T(8,128)}, f32[1,8,128,128]{3,2,1,0:T(8,128)S(1)}, u32[]{:S(2)}) copy-start(f32[1,8,128,128]{3,2,1,0:T(8,128)S(1)} %get-tuple-element.107) | copy-start | bytes 1572868
  20.4 13.0 %collective-permute-start.2 = (f32[8,128,128]{2,1,0:T(8,128)S(1)}, f32[8,128,128]{2,1,0:T(8,128)S(1)}, u32[]{:S(2)}, u32[]{:S(2)}) collective-permute-start(f32[8,128,128]{2,1,0:T(8,128)S(1)} %get-tuple-element.108), channel_id=1, source_target_pairs={{0,8},{8,0},{4,12},{12,4},{16,24},{24,16},{20,28},{28,20},{1,9},{9... | collective-permute-start | bytes 1572872 | tf_op jit(solution)/shard_map/ppermute | solution.py:21
  23.1 26.9 %copy-start.21 = (pred[256,256]{0,1:T(8,128)(4,1)}, pred[256,256]{0,1:T(8,128)(4,1)S(1)}, u32[]{:S(2)}) copy-start(pred[256,256]{0,1:T(8,128)(4,1)S(1)} %get-tuple-element.136) | copy-start | bytes 196612
  23.1 26.8 %copy-start.24 = (pred[256,256]{0,1:T(8,128)(4,1)}, pred[256,256]{0,1:T(8,128)(4,1)S(1)}, u32[]{:S(2)}) copy-start(pred[256,256]{0,1:T(8,128)(4,1)S(1)} %get-tuple-element.137) | copy-start | bytes 196612
  23.4 26.5 %copy-start.27 = (pred[256,256]{0,1:T(8,128)(4,1)}, pred[256,256]{0,1:T(8,128)(4,1)S(1)}, u32[]{:S(2)}) copy-start(pred[256,256]{0,1:T(8,128)(4,1)S(1)} %get-tuple-element.138) | copy-start | bytes 196612
  23.4 26.5 %copy-start.30 = (pred[256,256]{0,1:T(8,128)(4,1)}, pred[256,256]{0,1:T(8,128)(4,1)S(1)}, u32[]{:S(2)}) copy-start(pred[256,256]{0,1:T(8,128)(4,1)S(1)} %get-tuple-element.139) | copy-start | bytes 196612
  24.3 25.6 %copy-start.38 = (f32[8,256]{1,0:T(8,128)}, f32[8,256]{1,0:T(8,128)S(1)}, u32[]{:S(2)}) copy-start(f32[8,256]{1,0:T(8,128)S(1)} %get-tuple-element.111) | copy-start | bytes 24580
  24.3 25.6 %copy-start.41 = (f32[8,256]{1,0:T(8,128)}, f32[8,256]{1,0:T(8,128)S(1)}, u32[]{:S(2)}) copy-start(f32[8,256]{1,0:T(8,128)S(1)} %get-tuple-element.112) | copy-start | bytes 24580
  24.3 25.6 %copy-start.44 = (f32[8,256]{1,0:T(8,128)}, f32[8,256]{1,0:T(8,128)S(1)}, u32[]{:S(2)}) copy-start(f32[8,256]{1,0:T(8,128)S(1)} %get-tuple-element.113) | copy-start | bytes 24580
  24.3 25.6 %copy-start.47 = (f32[8,256]{1,0:T(8,128)}, f32[8,256]{1,0:T(8,128)S(1)}, u32[]{:S(2)}) copy-start(f32[8,256]{1,0:T(8,128)S(1)} %get-tuple-element.114) | copy-start | bytes 24580
  24.4 25.6 %copy-start.50 = (f32[8,256]{1,0:T(8,128)}, f32[8,256]{1,0:T(8,128)S(1)}, u32[]{:S(2)}) copy-start(f32[8,256]{1,0:T(8,128)S(1)} %get-tuple-element.115) | copy-start | bytes 24580
  24.4 25.6 %copy-start.53 = (f32[8,256]{1,0:T(8,128)}, f32[8,256]{1,0:T(8,128)S(1)}, u32[]{:S(2)}) copy-start(f32[8,256]{1,0:T(8,128)S(1)} %get-tuple-element.116) | copy-start | bytes 24580
  24.4 25.6 %copy-start.56 = (f32[8,256]{1,0:T(8,128)}, f32[8,256]{1,0:T(8,128)S(1)}, u32[]{:S(2)}) copy-start(f32[8,256]{1,0:T(8,128)S(1)} %get-tuple-element.117) | copy-start | bytes 24580
  24.4 25.6 %copy-start.59 = (f32[8,256]{1,0:T(8,128)}, f32[8,256]{1,0:T(8,128)S(1)}, u32[]{:S(2)}) copy-start(f32[8,256]{1,0:T(8,128)S(1)} %get-tuple-element.118) | copy-start | bytes 24580
  24.4 25.6 %copy-start.62 = (f32[8,256]{1,0:T(8,128)}, f32[8,256]{1,0:T(8,128)S(1)}, u32[]{:S(2)}) copy-start(f32[8,256]{1,0:T(8,128)S(1)} %get-tuple-element.119) | copy-start | bytes 24580
  33.6 12.8 %collective-permute-start.4 = (f32[8,128,128]{2,1,0:T(8,128)S(1)}, f32[8,128,128]{2,1,0:T(8,128)S(1)}, u32[]{:S(2)}, u32[]{:S(2)}) collective-permute-start(f32[8,128,128]{2,1,0:T(8,128)S(1)} %get-tuple-element.110), channel_id=1, source_target_pairs={{0,16},{16,0},{4,20},{20,4},{8,24},{24,8},{12,28},{28,12},{1,17},{... | collective-permute-start | bytes 1572872 | tf_op jit(solution)/shard_map/ppermute | solution.py:21
  35.8 9.9 %collective-permute-start.5 = (f32[8]{0:T(128)S(1)}, f32[8]{0:T(128)S(1)}, u32[]{:S(2)}, u32[]{:S(2)}) collective-permute-start(f32[8]{0:T(128)S(1)} %get-tuple-element.98), channel_id=1, source_target_pairs={{0,16},{16,0},{4,20},{20,4},{8,24},{24,8},{12,28},{28,12},{1,17},{... | collective-permute-start | bytes 104 | tf_op jit(solution)/shard_map/ppermute | solution.py:21
  103.2 48.2 %collective-permute-start.6 = (f32[8,128,128]{2,1,0:T(8,128)}, f32[8,128,128]{2,1,0:T(8,128)}, u32[]{:S(2)}, u32[]{:S(2)}) collective-permute-start(f32[8,128,128]{2,1,0:T(8,128)} %fusion.49), channel_id=1, source_target_pairs={{0,16},{16,0},{4,20},{20,4},{8,24},{24,8},{12,28},{28,12},{1,17},{... | collective-permute-start | bytes 1572872 | tf_op jit(solution)/shard_map/ppermute | solution.py:21
  152.7 13.7 %collective-permute-start.7 = (f32[8,128,128]{2,1,0:T(8,128)S(1)}, f32[8,128,128]{2,1,0:T(8,128)S(1)}, u32[]{:S(2)}, u32[]{:S(2)}) collective-permute-start(f32[8,128,128]{2,1,0:T(8,128)S(1)} %fusion.47), channel_id=1, source_target_pairs={{0,8},{8,0},{4,12},{12,4},{16,24},{24,16},{20,28},{28,20},{1,9},{9... | collective-permute-start | bytes 1572872 | tf_op jit(solution)/shard_map/ppermute | solution.py:21
  167.6 2.8 %collective-permute-start.8 = (f32[8,128,128]{2,1,0:T(8,128)S(1)}, f32[8,128,128]{2,1,0:T(8,128)S(1)}, u32[]{:S(2)}, u32[]{:S(2)}) collective-permute-start(f32[8,128,128]{2,1,0:T(8,128)S(1)} %get-tuple-element.95), channel_id=1, source_target_pairs={{0,4},{4,0},{8,12},{12,8},{16,20},{20,16},{24,28},{28,24},{1,5},{5... | collective-permute-start | bytes 1572872 | tf_op jit(solution)/shard_map/ppermute | solution.py:21
  (64 other events, 521.6 us)
where the time goes:
time: 175 us; the launch traced here: 174 us
  matrix products  45.1 us (26%)
  blocking collectives  34.6 us (20%)
  waiting for transfers between devices  31.7 us (18%)
  other arithmetic  26.7 us (15%)
  local copies, waits for them, and re-layouts  24.4 us (14%)
  starting transfers between devices  9.48 us (5%)
    ppermute x9, waiting for transfers between devices, partner(): return lax.ppermute(block, axis, route)  31.7 us
    psum x2, blocking collectives, local(): lax.psum((jnp.sum(gated * gated, axis=(0, 2)), jnp.sum(gated * scaled, ax...  21.8 us
    unnamed x172, local copies, waits for them, and re-layouts  20.6 us
    dot_general x1, matrix products, local(): gq_out = jnp.einsum('hli,lhik->hik', reach, pulled, precision=HIGH)  15.4 us
    psum x1, blocking collectives, local(): grad_gain = lax.psum(jnp.sum(grad_y * gated * inverse, axis=1), 'seq')  12.8 us
    ppermute x9, starting transfers between devices, partner(): return lax.ppermute(block, axis, route)  9.48 us
    unnamed x4, other arithmetic  8.11 us
    dot_general x1, matrix products, one_block(): jnp.einsum('hij,hjp->hip', mixing, values, preferred_element_type=jnp.flo...  4.99 us
  transfers between devices with their start and end apart: 9, of which 4 were waited for; matrix products, arithmetic and copies ran while one was open for 30% of the time, Pallas kernels for 0%

commit v1 on v0

v1 whole, which is shorter than its diff:
```python
import functools

import jax
import jax.numpy as jnp
from jax import lax
from jax.experimental import pallas as pl
from jax.experimental.pallas import tpu as pltpu
from jax.sharding import PartitionSpec as P

EPSILON = 1e-05
HIGH = lax.Precision.HIGHEST
F32 = jnp.float32
BF16 = jnp.bfloat16
PAD = 8


def nn(a, b, precision=None):
    return lax.dot_general(a, b, (((1,), (0,)), ((), ())), precision=precision, preferred_element_type=F32)


def nt(a, b, precision=None):
    return lax.dot_general(a, b, (((1,), (1,)), ((), ())), precision=precision, preferred_element_type=F32)


def tn(a, b, precision=None):
    return lax.dot_general(a, b, (((0,), (0,)), ((), ())), precision=precision, preferred_element_type=F32)


def kernel(
    levels, head_count, total,
    q_ref, k_ref, v_ref, ld_ref, lw_ref, z_ref, gain_ref, dy_ref,
    lo_ref, gq_ref, gk_ref, gv_ref, gl_ref, gz_ref, gg_ref,
    run_s, tail_s, runc_s, tailc_s, lev_s, own_s, oth_s, w_s, sd_s, mt_s, gst_s, qst_s, qt_s,
    mixed_s, bks_s, taken_s, fac_s, acc_s, nsend_s, nrecv_s, col_s, gx_s,
    e_s, er_s, bg_s, bgr_s, dmsg_s, dr_s, d_s, dfull_s, gkin_s, gvin_s, gsend_s, grecv_s,
    a_send, a_recv, f_send, n_send, n_recv, e_send, e_recv, b_send, b_recv,
    d_send, d_recv, h_send, h_recv, g_send, g_recv,
):
    heads, width, state = q_ref.shape
    hf = width // 2
    hh = heads // 2
    depth = width.bit_length() - 1
    me = lax.axis_index("seq")
    zed = lax.axis_index("head")
    core = me % 2

    def flip(bit):
        step = 1 << bit
        return me + step - 2 * step * ((me // step) % 2)

    def upper(bit):
        return (me // (1 << bit)) % 2 == 1

    mates = [flip(bit) for bit in range(levels)]
    sibling = mates[0]
    own_start = core * hh
    other_start = hh - own_start

    def rcopy(src, dst, ssem, rsem, target):
        return pltpu.make_async_remote_copy(
            src_ref=src, dst_ref=dst, send_sem=ssem, recv_sem=rsem,
            device_id=target, device_id_type=pl.DeviceIdType.MESH,
        )

    def state_copy(start, half):
        part = pl.ds(start, hh)
        return rcopy(own_s.at[0, part], oth_s.at[0, part], a_send.at[0, half], a_recv.at[0, half], {"seq": sibling})

    def link_copy(bit, i, target):
        h = own_start + i
        return rcopy(own_s.at[bit, h], oth_s.at[bit, h], a_send.at[bit, h], a_recv.at[bit, h], {"seq": target})

    def pass_copy(bit, h):
        return rcopy(oth_s.at[bit, h], oth_s.at[bit, h], f_send.at[bit, h], a_recv.at[bit, h], {"seq": sibling})

    def norm_copy(d):
        peer = lax.rem(zed + d, head_count)
        return rcopy(nsend_s, nrecv_s.at[d - 1], n_send.at[d - 1], n_recv.at[d - 1], {"head": peer})

    def e_copy():
        return rcopy(e_s.at[pl.ds(other_start, hh)], er_s, e_send, e_recv, {"seq": sibling})

    def bg_copy():
        return rcopy(bg_s, bgr_s, b_send, b_recv, {"seq": sibling})

    def d_copy(bit, i, target):
        return rcopy(dmsg_s.at[bit, i], dr_s.at[bit, i], d_send.at[bit, i], d_recv.at[bit, i], {"seq": target})

    def half_copy(h):
        return rcopy(dfull_s.at[h], dfull_s.at[h], h_send.at[h], h_recv.at[h], {"seq": sibling})

    def gain_copy(bit):
        return rcopy(gsend_s.at[bit], grecv_s.at[bit], g_send.at[bit], g_recv.at[bit], {"seq": mates[bit]})

    barrier = pltpu.get_barrier_semaphore()
    for mate in mates:
        pl.semaphore_signal(barrier, inc=1, device_id={"seq": mate}, device_id_type=pl.DeviceIdType.MESH)
    for d in range(1, head_count):
        peer = lax.rem(zed + d, head_count)
        pl.semaphore_signal(barrier, inc=1, device_id={"head": peer}, device_id_type=pl.DeviceIdType.MESH)

    low = lax.broadcasted_iota(jnp.int32, (width, width), 0)
    high = lax.broadcasted_iota(jnp.int32, (width, width), 1)
    running = nn(ld_ref[...], jnp.where(low <= high, 1.0, 0.0), HIGH)
    ending = jnp.broadcast_to(running[:, width - 1 : width], (heads, width))
    tail = jnp.exp(ending - running)
    running_c = running.T
    tail_c = tail.T
    for h in range(heads):
        run_s[h] = running[h : h + 1]
        tail_s[h] = tail[h : h + 1]
        runc_s[h] = jnp.broadcast_to(running_c[:, h : h + 1], (width, hf))
        tailc_s[h] = jnp.broadcast_to(tail_c[:, h : h + 1], (width, hf))
        own_s[0, h, state:] = jnp.broadcast_to(ending[h : h + 1, :hf], (PAD, hf))

    row = lax.broadcasted_iota(jnp.int32, (hf, hf), 0)
    column = lax.broadcasted_iota(jnp.int32, (hf, hf), 1)
    crossed = jnp.bitwise_xor(row, column)
    level = jnp.zeros((hf, hf), jnp.int32)
    for shift in range(depth - 1):
        level = level + jnp.where(crossed >= (1 << shift), 1, 0)
    lev_s[...] = jnp.where(row <= column, level, -1)
    gst_s[hf:, :hf] = jnp.zeros((hf, hf), BF16)
    acc_s[...] = jnp.zeros_like(acc_s)

    def own_state(h):
        scaled = (k_ref[h].astype(F32) * tailc_s[h]).astype(BF16)
        own_s[0, h, :state] = tn(scaled, v_ref[h])

    @pl.loop(0, hh)
    def _(i):
        own_state(other_start + i)

    pl.semaphore_wait(barrier, levels + head_count - 1)
    state_copy(other_start, 0).start()

    @pl.loop(0, hh)
    def _(i):
        own_state(own_start + i)

    state_copy(own_start, 1).start()

    def forward(h):
        q, k, v = q_ref[h], k_ref[h], v_ref[h]
        run, runc, lw = run_s[h], runc_s[h], lw_ref[h]
        lev = lev_s[...]
        top = nt(k[:hf], q)
        low_scores = nt(k[hf:], q[hf:])

        def diagonal(place, scores, lo):
            spread = jnp.where(lev >= 0, run[:, lo : lo + hf] - runc[lo : lo + hf], 0.0)
            decay = jnp.exp(spread)
            chosen = jnp.where(lev == 0, lw[0:1, lo : lo + hf], 0.0)
            for step in range(1, depth):
                chosen = jnp.where(lev == step, lw[step : step + 1, lo : lo + hf], chosen)
            weight = decay * chosen
            w_s[h, place] = weight
            sd_s[h, place] = scores * decay
            mt_s[h, lo : lo + hf, lo : lo + hf] = (scores * weight).astype(BF16)

        diagonal(0, top[:, :hf], 0)
        diagonal(2, low_scores, hf)
        decay = jnp.exp(run[:, hf:] - runc[:hf])
        weight = decay * lw[depth : depth + 1, hf:]
        scores = top[:, hf:]
        w_s[h, 1] = weight
        sd_s[h, 1] = scores * decay
        mt_s[h, :hf, hf:] = (scores * weight).astype(BF16)
        mt_s[h, hf:, :hf] = jnp.zeros((hf, hf), BF16)
        mixed_s[h] = tn(mt_s[h], v)
        qt = q.astype(F32).T
        qt_s[h] = qt
        reach = lw[depth + 1 : depth + 1 + levels] * jnp.exp(run)
        for bit in range(levels):
            qst_s[h, bit * state : (bit + 1) * state] = (qt * reach[bit : bit + 1]).astype(BF16)

    def merge(bit, i):
        h = own_start + i
        mine, theirs = own_s[bit, h], oth_s[bit, h]
        own_rate, other_rate = mine[state : state + 1], theirs[state : state + 1]
        own_f = jnp.where(upper(bit), 1.0, jnp.exp(other_rate))
        other_f = jnp.where(upper(bit), jnp.exp(own_rate), 1.0)
        own_s[bit + 1, h, :state] = own_f * mine[:state] + other_f * theirs[:state]
        own_s[bit + 1, h, state:] = mine[state:] + theirs[state:]

    lead = min(2, heads)

    @pl.loop(0, lead)
    def _(h):
        forward(h)

    state_copy(own_start, 0).wait_recv()
    state_copy(own_start, 1).wait_recv()
    if levels > 1:

        @pl.loop(0, hh)
        def _(i):
            merge(0, i)
            link_copy(1, i, mates[1]).start()

    done = lead
    for bit in range(1, levels - 1):
        upto = min(heads, done + 2)

        @pl.loop(done, upto)
        def _(h):
            forward(h)

        done = upto
        ahead_of = min(heads - done, hh)

        @pl.loop(0, hh)
        def _(i, bit=bit, done=done, ahead_of=ahead_of):
            link_copy(bit, i, mates[bit]).wait_recv()
            merge(bit, i)
            link_copy(bit + 1, i, mates[bit + 1]).start()
            pass_copy(bit, own_start + i).start()

            @pl.when(i < ahead_of)
            def _():
                forward(done + i)

        done += ahead_of

    if done < heads:

        @pl.loop(done, heads)
        def _(h):
            forward(h)

    def outer(h):
        ahead = jnp.zeros((1, state), F32)
        for bit in range(levels):
            taken = jnp.where(upper(bit), jnp.exp(ahead), 0.0)
            taken_s[bit, h] = taken
            bks_s[h, bit * state : (bit + 1) * state] = (taken * oth_s[bit, h, :state]).astype(BF16)
            ahead = ahead + jnp.where(upper(bit), oth_s[bit, h, state : state + 1], 0.0)
        mixed = mixed_s[h] + tn(qst_s[h], bks_s[h])
        mixed_s[h] = mixed
        z = z_ref[h].astype(F32)
        gated = mixed * (z * jax.nn.sigmoid(z))
        scaled = dy_ref[h].astype(F32) * gain_ref[pl.ds(h, 1), :]
        acc_s[0] += gated * gated
        acc_s[1] += gated * scaled

    @pl.loop(0, hh)
    def _(i):
        h = own_start + i
        if levels > 1:
            link_copy(levels - 1, i, mates[levels - 1]).wait_recv()
            pass_copy(levels - 1, h).start()
        outer(h)

    @pl.loop(0, hh)
    def _(i):
        h = other_start + i
        for bit in range(1, levels):
            pass_copy(bit, h).wait_recv()
        outer(h)

    pick = lax.broadcasted_iota(jnp.int32, (8, state), 0)
    sums = nt(jnp.where(pick == 0, 1.0, 0.0), acc_s[0], HIGH) + nt(jnp.where(pick == 1, 1.0, 0.0), acc_s[1], HIGH)
    nsend_s[...] = sums
    for d in range(1, head_count):
        norm_copy(d).start()
    for d in range(1, head_count):
        norm_copy(d).wait_recv()
        sums = sums + nrecv_s[d - 1]
    inverse = lax.rsqrt(sums[0:1] / total + EPSILON)
    pull = inverse * inverse * inverse * sums[1:2] / total
    columns = jnp.where(lax.broadcasted_iota(jnp.int32, (8, width), 0) == 0, inverse, pull).T
    col_s[0] = jnp.broadcast_to(columns[:, 0:1], (width, state))
    col_s[1] = jnp.broadcast_to(columns[:, 1:2], (width, state))

    def gate_back(h):
        z = z_ref[h].astype(F32)
        sig = jax.nn.sigmoid(z)
        act = z * sig
        mixed = mixed_s[h]
        gated = mixed * act
        gain = gain_ref[pl.ds(h, 1), :]
        dy = dy_ref[h].astype(F32)
        inv = col_s[0]
        normed = gated * inv
        lo_ref[h] = (gain * normed).astype(BF16)
        gsend_s[0, pl.ds(h, 1), :] = jnp.sum(dy * normed, axis=0, keepdims=True)
        grad = inv * (dy * gain) - gated * col_s[1]
        gz_ref[h] = (grad * mixed * sig * (1.0 + z * (1.0 - sig))).astype(BF16)
        gx = (grad * act).astype(BF16)
        gx_s[h] = gx
        grads = nn(qst_s[h], gx)
        bg_s[h] = taken_s[0, h] * grads[:state]
        for bit in range(1, levels):
            e_s[h, bit - 1] = taken_s[bit, h] * grads[bit * state : (bit + 1) * state]

    @pl.loop(0, hh)
    def _(i):
        gate_back(other_start + i)

    if levels > 1:
        e_copy().start()

    @pl.loop(0, hh)
    def _(i):
        gate_back(own_start + i)

    bg_copy().start()
    gain_copy(0).start()

    def send_down(bit, i):
        h = own_start + i
        e = e_s[h, bit - 1] + er_s[i, bit - 1]
        if bit < levels - 1:
            rate, other_rate = own_s[bit, h, state : state + 1], oth_s[bit, h, state : state + 1]
            other_f = jnp.where(upper(bit), jnp.exp(rate), 1.0)
            e = e + other_f * d_s[i]
        dmsg_s[bit, i] = e
        d_copy(bit, i, mates[bit]).start()

    def take_down(bit, i):
        h = own_start + i
        d_copy(bit, i, mates[bit]).wait_recv()
        got = dr_s[bit, i]
        if bit < levels - 1:
            other_rate = oth_s[bit, h, state : state + 1]
            own_f = jnp.where(upper(bit), 1.0, jnp.exp(other_rate))
            got = got + own_f * d_s[i]
        if bit > 1:
            d_s[i] = got
        else:
            dfull_s[h] = got

    if levels > 1:
        e_copy().wait_recv()

        @pl.loop(0, hh)
        def _(i):
            send_down(levels - 1, i)
    else:
        dfull_s[...] = jnp.zeros_like(dfull_s)

    def block_grads(h):
        q, k, v, gx = q_ref[h], k_ref[h], v_ref[h], gx_s[h]
        lev = lev_s[...]
        top = nt(v[:hf], gx)
        low_grads = nt(v[hf:], gx[hf:])
        for place, part, lo in ((0, top[:, :hf], 0), (2, low_grads, hf)):
            gst_s[lo : lo + hf, lo : lo + hf] = (part * w_s[h, place]).astype(BF16)
            moved = part * sd_s[h, place]
            for step in range(depth):
                gl_ref[h, step : step + 1, lo : lo + hf] = jnp.sum(
                    jnp.where(lev == step, moved, 0.0), axis=0, keepdims=True
                )
        part = top[:, hf:]
        gst_s[:hf, hf:] = (part * w_s[h, 1]).astype(BF16)
        gl_ref[h, depth : depth + 1, :hf] = jnp.zeros((1, hf), F32)
        gl_ref[h, depth : depth + 1, hf:] = jnp.sum(part * sd_s[h, 1], axis=0, keepdims=True)
        gst = gst_s[...]
        gkin_s[h] = nn(gst, q)
        gvin_s[h] = nn(mt_s[h], gx)
        gqt = tn(k, gst)
        pulled = nt(bks_s[h], gx)
        exp_run = jnp.exp(run_s[h])
        qt = qt_s[h]
        for bit in range(levels):
            here = pulled[bit * state : (bit + 1) * state]
            at = depth + 1 + bit
            gl_ref[h, at : at + 1, :] = exp_run * jnp.sum(qt * here, axis=0, keepdims=True)
            gqt = gqt + (lw_ref[h, at : at + 1, :] * exp_run) * here
        rest = depth + 1 + levels
        gl_ref[h, rest:, :] = jnp.zeros((lw_ref.shape[1] - rest, width), F32)
        gq_ref[h] = gqt.T.astype(BF16)

    done = 0
    for bit in range(levels - 1, 0, -1):
        upto = min(heads, done + 2)

        @pl.loop(done, upto)
        def _(h):
            block_grads(h)

        done = upto
        ahead_of = min(heads - done, hh)
        turn = levels - 1 - bit
        gain_copy(turn).wait_recv()
        gsend_s[turn + 1] = gsend_s[turn] + grecv_s[turn]
        gain_copy(turn + 1).start()

        @pl.loop(0, hh)
        def _(i, bit=bit, done=done, ahead_of=ahead_of):
            take_down(bit, i)
            if bit > 1:
                send_down(bit - 1, i)
            else:
                half_copy(own_start + i).start()

            @pl.when(i < ahead_of)
            def _():
                block_grads(done + i)

        done += ahead_of

    if done < heads:

        @pl.loop(done, heads)
        def _(h):
            block_grads(h)

    gain_copy(levels - 1).wait_recv()
    gg_ref[...] = gsend_s[levels - 1] + grecv_s[levels - 1]
    bg_copy().wait_recv()

    def finish(h):
        own_f = jnp.where(upper(0), 1.0, jnp.exp(oth_s[0, h, state : state + 1]))
        down = (own_f * dfull_s[h] + bgr_s[h]).astype(BF16)
        tail = tailc_s[h]
        gk_ref[h] = (gkin_s[h] + tail * nt(v_ref[h], down)).astype(BF16)
        gv_ref[h] = (gvin_s[h] + tail * nn(k_ref[h], down)).astype(BF16)

    @pl.loop(0, hh)
    def _(i):
        finish(own_start + i)

    @pl.loop(0, hh)
    def _(i):
        h = other_start + i
        if levels > 1:
            half_copy(h).wait_recv()
        finish(h)

    state_copy(other_start, 0).wait_send()
    state_copy(own_start, 1).wait_send()
    bg_copy().wait_send()
    for d in range(1, head_count):
        norm_copy(d).wait_send()
    for bit in range(levels):
        gain_copy(bit).wait_send()
    if levels > 1:
        e_copy().wait_send()

        @pl.loop(0, hh)
        def _(i):
            half_copy(own_start + i).wait_send()
            for bit in range(1, levels):
                link_copy(bit, i, mates[bit]).wait_send()
                pass_copy(bit, own_start + i).wait_send()
                d_copy(bit, i, mates[bit]).wait_send()


def local(levels, head_count, queries, keys, values, log_decay, level_weight, gate_input, norm_gain, out_grad):
    heads, width, state = queries.shape
    feature = values.shape[2]
    hf, hh = width // 2, heads // 2
    total = heads * head_count * feature
    tokens = jax.ShapeDtypeStruct(queries.shape, BF16)
    vmem = pl.BlockSpec(memory_space=pltpu.VMEM)

    def f32(*shape):
        return pltpu.VMEM(shape, F32)

    def bf16(*shape):
        return pltpu.VMEM(shape, BF16)

    dma = pltpu.SemaphoreType.DMA
    more = max(levels - 1, 1)
    scratch = [
        f32(heads, 1, width), f32(heads, 1, width), f32(heads, width, hf), f32(heads, width, hf),
        pltpu.VMEM((hf, hf), jnp.int32),
        f32(levels, heads, state + PAD, feature), f32(levels, heads, state + PAD, feature),
        f32(heads, 3, hf, hf), f32(heads, 3, hf, hf), bf16(heads, width, width), bf16(width, width),
        bf16(heads, levels * state, width), f32(heads, state, width),
        f32(heads, width, feature), bf16(heads, levels * state, feature), f32(levels, heads, 1, feature),
        f32(8, 128), f32(2, width, feature), f32(8, width), f32(max(head_count - 1, 1), 8, width),
        f32(2, width, feature), bf16(heads, width, feature),
        f32(heads, more, state, feature), f32(hh, more, state, feature),
        f32(heads, state, feature), f32(heads, state, feature),
        f32(levels, hh, state, feature), f32(levels, hh, state, feature), f32(hh, state, feature),
        f32(heads, state, feature), f32(heads, width, state), f32(heads, width, feature),
        f32(levels, heads, feature), f32(levels, heads, feature),
        dma((levels, heads)), dma((levels, heads)), dma((levels, heads)),
        dma((max(head_count - 1, 1),)), dma((max(head_count - 1, 1),)), dma, dma, dma, dma,
        dma((levels, hh)), dma((levels, hh)), dma((heads,)), dma((heads,)), dma((levels,)), dma((levels,)),
    ]
    return pl.pallas_call(
        functools.partial(kernel, levels, head_count, total),
        out_shape=(
            tokens, tokens, tokens, tokens,
            jax.ShapeDtypeStruct(level_weight.shape, F32), tokens,
            jax.ShapeDtypeStruct(norm_gain.shape, F32),
        ),
        in_specs=[vmem] * 8,
        out_specs=(vmem,) * 7,
        scratch_shapes=scratch,
        compiler_params=pltpu.CompilerParams(
            collective_id=0, has_side_effects=True, vmem_limit_bytes=48 * 1024 * 1024
        ),
    )(queries, keys, values, log_decay, level_weight, gate_input, norm_gain, out_grad)


def solution(mesh):
    levels = mesh.shape["seq"].bit_length() - 1
    tokens = P("head", "seq", None)
    in_specs = (tokens, tokens, tokens, P("head", "seq"), P("head", None, "seq"), tokens, P("head", None), tokens)
    out_specs = (tokens, tokens, tokens, tokens, P("head", None, "seq"), tokens, P("head", None))
    return jax.shard_map(
        functools.partial(local, levels, mesh.shape["head"]),
        mesh=mesh, in_specs=in_specs, out_specs=out_specs, check_vma=False,
    )
```

time: 175 us -> 55.7 us (0.32)
  matrix products: 45.1 us -> 0 us
  Pallas kernels: 0 us -> 43.1 us
  blocking collectives: 34.6 us -> 0 us
  waiting for transfers between devices: 31.7 us -> 0 us
  other arithmetic: 26.7 us -> 0 us
  local copies, waits for them, and re-layouts: 24.4 us -> 11.5 us
  starting transfers between devices: 9.48 us -> 0 us
    dot_general x13 -> x0, matrix products: 45.1 us -> none  [the longest x1 15.4 us: local(): gq_out = jnp.einsum('hli,lhik->hik', reach, pulled, precision=HIGH)]
    pallas_call x0 -> x1, Pallas kernels: none -> 43.1 us  [local(): pl.pallas_call(functools.partial(kernel, levels, head_count, total), out_...]
    psum x3 -> x0, blocking collectives: 34.6 us -> none  [the longest x2 21.8 us: local(): lax.psum((jnp.sum(gated * gated, axis=(0, 2)), jnp.sum(gated * scaled, ax...]
    ppermute x9 -> x0, waiting for transfers between devices: 31.7 us -> none  [partner(): return lax.ppermute(block, axis, route)]
    unnamed x172 -> x21, local copies, waits for them, and re-layouts: 20.6 us -> 10.8 us
    ppermute x9 -> x0, starting transfers between devices: 9.48 us -> none  [partner(): return lax.ppermute(block, axis, route)]
    unnamed x4 -> x0, other arithmetic: 8.11 us -> none
    reduce_sum x2 -> x0, other arithmetic: 6.38 us -> none  [the longest x1 3.96 us: one_block(): jnp.sum(jnp.where((level == place)[None], moved, 0.0), axis=2)]
  transfers between devices with their start and end apart: 9 -> 0, of which waited for: 4 -> 0; matrix products, arithmetic and copies ran while one was open for 30% -> 0% of each run, Pallas kernels for 0% -> 0%
where the time goes in v1:
time: 55.7 us; the launch traced here: 55.3 us
  Pallas kernels  43.1 us (77%)
  local copies, waits for them, and re-layouts  11.5 us (21%)
  between operations  0.69 us (1%)
    pallas_call x1, Pallas kernels, local(): pl.pallas_call(functools.partial(kernel, levels, head_count, total), out_...  43.1 us
    unnamed x21, local copies, waits for them, and re-layouts  10.8 us

profile of v1, /device:TPU:0, one launch (start us, length us, event | category | flops | bytes accessed | tf_op | source)
XLA Modules:
  0.0 55.3 jit_solution(2693381927314290939)
XLA Ops:
  0.6 0.0 copy-start.6
  0.6 0.0 copy-start.5
  0.7 1.0 %copy.15.lw_ref = f32[8,21,256]{2,1,0:T(8,128)S(1)} copy(f32[8,21,256]{2,0,1:T(8,128)} %param.12) | data formatting | bytes 344064 | tf_op args[4]
  1.6 0.0 copy-done.6
  1.7 0.0 copy-done.5
  1.7 0.0 copy-start
  1.7 1.0 %copy-done = bf16[8,256,128]{2,1,0:T(8,128)(2,1)S(1)} copy-done((bf16[8,256,128]{2,1,0:T(8,128)(2,1)S(1)}, bf16[8,256,128]{2,1,0:T(8,128)(2,1)}, u32[]{:S(2)}) %copy-start) | copy-done | bytes 524312
  2.7 0.0 copy-start.1
  2.7 1.0 %copy-done.1 = bf16[8,256,128]{2,1,0:T(8,128)(2,1)S(1)} copy-done((bf16[8,256,128]{2,1,0:T(8,128)(2,1)S(1)}, bf16[8,256,128]{2,1,0:T(8,128)(2,1)}, u32[]{:S(2)}) %copy-start.1) | copy-done | bytes 524312
  3.8 0.0 copy-start.2
  3.8 1.0 %copy-done.2 = bf16[8,256,128]{2,1,0:T(8,128)(2,1)S(1)} copy-done((bf16[8,256,128]{2,1,0:T(8,128)(2,1)S(1)}, bf16[8,256,128]{2,1,0:T(8,128)(2,1)}, u32[]{:S(2)}) %copy-start.2) | copy-done | bytes 524312
  4.8 0.0 copy-start.3
  4.8 1.0 %copy-done.3 = bf16[8,256,128]{2,1,0:T(8,128)(2,1)S(1)} copy-done((bf16[8,256,128]{2,1,0:T(8,128)(2,1)S(1)}, bf16[8,256,128]{2,1,0:T(8,128)(2,1)}, u32[]{:S(2)}) %copy-start.3) | copy-done | bytes 524312
  5.8 0.0 copy-start.4
  5.8 1.0 %copy-done.4 = bf16[8,256,128]{2,1,0:T(8,128)(2,1)S(1)} copy-done((bf16[8,256,128]{2,1,0:T(8,128)(2,1)S(1)}, bf16[8,256,128]{2,1,0:T(8,128)(2,1)}, u32[]{:S(2)}) %copy-start.4) | copy-done | bytes 524312
  6.9 43.1 %shard_map.135 = (bf16[8,256,128]{2,1,0:T(8,128)(2,1)S(1)}, bf16[8,256,128]{2,1,0:T(8,128)(2,1)S(1)}, bf16[8,256,128]{2,1,0:T(8,128)(2,1)S(1)}, bf16[8,256,128]{...) custom-call(bf16[8,256,128]{2,1,0:T(8,128)(2,1)S(1)} %copy-done, ...), custom_call_target="tpu_custom_call" | custom-call | tf_op jit(solution)/shard_map/pallas_call | solution.py:484
  50.0 0.7 %copy.16 = f32[8,21,256]{2,0,1:T(8,128)} copy(f32[8,21,256]{2,1,0:T(8,128)S(1)} %get-tuple-element.11) | data formatting | bytes 344064 | tf_op jit(solution)/shard_map/pallas_call | solution.py:484
  50.7 0.8 %copy.23 = bf16[8,256,128]{2,1,0:T(8,128)(2,1)} copy(bf16[8,256,128]{2,1,0:T(8,128)(2,1)S(1)} %get-tuple-element.21) | data formatting | bytes 1048576
  51.5 0.8 %copy.24 = bf16[8,256,128]{2,1,0:T(8,128)(2,1)} copy(bf16[8,256,128]{2,1,0:T(8,128)(2,1)S(1)} %get-tuple-element.22) | data formatting | bytes 1048576
  52.3 0.8 %copy.25 = bf16[8,256,128]{2,1,0:T(8,128)(2,1)} copy(bf16[8,256,128]{2,1,0:T(8,128)(2,1)S(1)} %get-tuple-element.23) | data formatting | bytes 1048576
  53.1 0.8 %copy.26 = bf16[8,256,128]{2,1,0:T(8,128)(2,1)} copy(bf16[8,256,128]{2,1,0:T(8,128)(2,1)S(1)} %get-tuple-element.24) | data formatting | bytes 1048576
  53.9 0.8 %copy.27 = bf16[8,256,128]{2,1,0:T(8,128)(2,1)} copy(bf16[8,256,128]{2,1,0:T(8,128)(2,1)S(1)} %get-tuple-element.26) | data formatting | bytes 1048576
  54.7 0.6 %copy.28 = f32[8,128]{1,0:T(8,128)} copy(f32[8,128]{1,0:T(8,128)S(1)} %get-tuple-element.27) | data formatting | bytes 8192
Async XLA Ops:
  0.6 1.0 %copy-start.6 = (f32[8,128]{1,0:T(8,128)S(1)}, f32[8,128]{1,0:T(8,128)}, u32[]{:S(2)}) copy-start(f32[8,128]{1,0:T(8,128)} %gain_ref.1) | copy-start | bytes 12292
  0.6 1.0 %copy-start.5 = (f32[8,256]{1,0:T(8,128)S(1)}, f32[8,256]{1,0:T(8,128)}, u32[]{:S(2)}) copy-start(f32[8,256]{1,0:T(8,128)} %ld_ref.1) | copy-start | bytes 24580
  1.7 1.0 %copy-start = (bf16[8,256,128]{2,1,0:T(8,128)(2,1)S(1)}, bf16[8,256,128]{2,1,0:T(8,128)(2,1)}, u32[]{:S(2)}) copy-start(bf16[8,256,128]{2,1,0:T(8,128)(2,1)} %q_ref.1) | copy-start | bytes 1572868
  2.7 1.0 %copy-start.1 = (bf16[8,256,128]{2,1,0:T(8,128)(2,1)S(1)}, bf16[8,256,128]{2,1,0:T(8,128)(2,1)}, u32[]{:S(2)}) copy-start(bf16[8,256,128]{2,1,0:T(8,128)(2,1)} %k_ref.1) | copy-start | bytes 1572868
  3.8 1.0 %copy-start.2 = (bf16[8,256,128]{2,1,0:T(8,128)(2,1)S(1)}, bf16[8,256,128]{2,1,0:T(8,128)(2,1)}, u32[]{:S(2)}) copy-start(bf16[8,256,128]{2,1,0:T(8,128)(2,1)} %v_ref.1) | copy-start | bytes 1572868
  4.8 1.0 %copy-start.3 = (bf16[8,256,128]{2,1,0:T(8,128)(2,1)S(1)}, bf16[8,256,128]{2,1,0:T(8,128)(2,1)}, u32[]{:S(2)}) copy-start(bf16[8,256,128]{2,1,0:T(8,128)(2,1)} %z_ref.1) | copy-start | bytes 1572868
  5.8 1.0 %copy-start.4 = (bf16[8,256,128]{2,1,0:T(8,128)(2,1)S(1)}, bf16[8,256,128]{2,1,0:T(8,128)(2,1)}, u32[]{:S(2)}) copy-start(bf16[8,256,128]{2,1,0:T(8,128)(2,1)} %dy_ref.1) | copy-start | bytes 1572868

commit v2 on v1

v2 whole, which is shorter than its diff:
```python
import functools

import jax
import jax.numpy as jnp
from jax import lax
from jax.experimental import pallas as pl
from jax.experimental.pallas import tpu as pltpu
from jax.sharding import PartitionSpec as P

EPSILON = 1e-05
HIGH = lax.Precision.HIGHEST
F32 = jnp.float32
BF16 = jnp.bfloat16
PAD = 8


def nn(a, b, precision=None):
    return lax.dot_general(a, b, (((1,), (0,)), ((), ())), precision=precision, preferred_element_type=F32)


def nt(a, b, precision=None):
    return lax.dot_general(a, b, (((1,), (1,)), ((), ())), precision=precision, preferred_element_type=F32)


def tn(a, b, precision=None):
    return lax.dot_general(a, b, (((0,), (0,)), ((), ())), precision=precision, preferred_element_type=F32)


def kernel(
    levels, head_count, total,
    q_in, k_in, v_in, ld_in, lw_in, z_in, gain_in, dy_in,
    lo_ref, gq_ref, gk_ref, gv_ref, gl_ref, gz_ref, gg_ref,
    k_ref, v_ref, gkin_s, gvin_s, tailc_s, q_ref, ld_ref, lw_ref, z_ref, gain_ref, dy_ref,
    run_s, tail_s, runc_s, lev_s, own_s, oth_s, w_s, sd_s, mt_s, qst_s, qt_s,
    mixed_s, bks_s, taken_s, acc_s, nsend_s, nrecv_s, col_s, gx_s,
    e_s, er_s, bg_s, bgr_s, dmsg_s, dr_s, d_s, dfull_s, gsend_s, grecv_s,
    in_sem,
    a_send, a_recv, f_send, n_send, n_recv, e_send, e_recv, b_send, b_recv,
    d_send, d_recv, h_send, h_recv, g_send, g_recv,
):
    heads, width, state = q_ref.shape
    hf = width // 2
    hh = heads // 2
    depth = width.bit_length() - 1
    me = lax.axis_index("seq")
    zed = lax.axis_index("head")
    core = me % 2

    def flip(bit):
        step = 1 << bit
        return me + step - 2 * step * ((me // step) % 2)

    def upper(bit):
        return (me // (1 << bit)) % 2 == 1

    mates = [flip(bit) for bit in range(levels)]
    sibling = mates[0]
    own_start = core * hh
    other_start = hh - own_start

    def rcopy(src, dst, ssem, rsem, target):
        return pltpu.make_async_remote_copy(
            src_ref=src, dst_ref=dst, send_sem=ssem, recv_sem=rsem,
            device_id=target, device_id_type=pl.DeviceIdType.MESH,
        )

    def state_copy(start, half):
        part = pl.ds(start, hh)
        return rcopy(own_s.at[0, part], oth_s.at[0, part], a_send.at[0, half], a_recv.at[0, half], {"seq": sibling})

    def link_copy(bit, i, target):
        h = own_start + i
        return rcopy(own_s.at[bit, h], oth_s.at[bit, h], a_send.at[bit, h], a_recv.at[bit, h], {"seq": target})

    def pass_copy(bit, h):
        return rcopy(oth_s.at[bit, h], oth_s.at[bit, h], f_send.at[bit, h], a_recv.at[bit, h], {"seq": sibling})

    def norm_copy(d):
        peer = lax.rem(zed + d, head_count)
        return rcopy(nsend_s, nrecv_s.at[d - 1], n_send.at[d - 1], n_recv.at[d - 1], {"head": peer})

    def e_copy():
        return rcopy(e_s.at[pl.ds(other_start, hh)], er_s, e_send, e_recv, {"seq": sibling})

    def bg_copy():
        return rcopy(bg_s, bgr_s, b_send, b_recv, {"seq": sibling})

    def d_copy(bit, i, target):
        return rcopy(dmsg_s.at[bit, i], dr_s.at[bit, i], d_send.at[bit, i], d_recv.at[bit, i], {"seq": target})

    def half_copy(h):
        return rcopy(dfull_s.at[h], dfull_s.at[h], h_send.at[h], h_recv.at[h], {"seq": sibling})

    def gain_copy(bit):
        return rcopy(gsend_s.at[bit], grecv_s.at[bit], g_send.at[bit], g_recv.at[bit], {"seq": mates[bit]})

    loads = [
        pltpu.make_async_copy(src, dst, in_sem.at[at])
        for at, (src, dst) in enumerate(
            [(ld_in, ld_ref), (k_in, k_ref), (v_in, v_ref), (q_in, q_ref), (lw_in, lw_ref),
             (z_in, z_ref), (dy_in, dy_ref), (gain_in, gain_ref)]
        )
    ]
    for load in loads:
        load.start()
    group = 2 if hh % 2 == 0 else 1

    def together(work, places):
        for store in [work(place) for place in places]:
            store()

    def sweep(work, start, count):
        @pl.loop(0, count // group)
        def _(i):
            together(work, [start + group * i + n for n in range(group)])

    barrier = pltpu.get_barrier_semaphore()
    for mate in mates:
        pl.semaphore_signal(barrier, inc=1, device_id={"seq": mate}, device_id_type=pl.DeviceIdType.MESH)
    for d in range(1, head_count):
        peer = lax.rem(zed + d, head_count)
        pl.semaphore_signal(barrier, inc=1, device_id={"head": peer}, device_id_type=pl.DeviceIdType.MESH)

    loads[0].wait()

    low = lax.broadcasted_iota(jnp.int32, (width, width), 0)
    high = lax.broadcasted_iota(jnp.int32, (width, width), 1)
    running = nn(ld_ref[...], jnp.where(low <= high, 1.0, 0.0), HIGH)
    ending = jnp.broadcast_to(running[:, width - 1 : width], (heads, width))
    tail = jnp.exp(ending - running)
    running_c = running.T
    tail_c = tail.T
    for h in range(heads):
        run_s[h] = running[h : h + 1]
        tail_s[h] = tail[h : h + 1]
        runc_s[h] = jnp.broadcast_to(running_c[:, h : h + 1], (width, hf))
        tailc_s[h] = jnp.broadcast_to(tail_c[:, h : h + 1], (width, hf))
        own_s[0, h, state:] = jnp.broadcast_to(ending[h : h + 1, :hf], (PAD, hf))

    row = lax.broadcasted_iota(jnp.int32, (hf, hf), 0)
    column = lax.broadcasted_iota(jnp.int32, (hf, hf), 1)
    crossed = jnp.bitwise_xor(row, column)
    level = jnp.zeros((hf, hf), jnp.int32)
    for shift in range(depth - 1):
        level = level + jnp.where(crossed >= (1 << shift), 1, 0)
    lev_s[...] = jnp.where(row <= column, level, -1)
    acc_s[...] = jnp.zeros_like(acc_s)

    def own_state(h):
        scaled = (k_ref[h].astype(F32) * tailc_s[h]).astype(BF16)
        summed = tn(scaled, v_ref[h])

        def store():
            own_s[0, h, :state] = summed

        return store

    loads[1].wait()
    loads[2].wait()
    sweep(own_state, other_start, hh)
    pl.semaphore_wait(barrier, levels + head_count - 1)
    state_copy(other_start, 0).start()

    sweep(own_state, own_start, hh)
    state_copy(own_start, 1).start()
    loads[3].wait()
    loads[4].wait()

    def forward(h):
        q, k, v = q_ref[h], k_ref[h], v_ref[h]
        run, runc = run_s[h], runc_s[h]
        lw = [lw_ref[step, pl.ds(h, 1), :] for step in range(depth + 1 + levels)]
        lev = lev_s[...]
        top = nt(k[:hf], q)
        low_scores = nt(k[hf:], q[hf:])

        def diagonal(scores, lo):
            spread = jnp.where(lev >= 0, run[:, lo : lo + hf] - runc[lo : lo + hf], 0.0)
            decay = jnp.exp(spread)
            chosen = jnp.where(lev == 0, lw[0][:, lo : lo + hf], 0.0)
            for step in range(1, depth):
                chosen = jnp.where(lev == step, lw[step][:, lo : lo + hf], chosen)
            weight = decay * chosen
            return weight, scores * decay, (scores * weight).astype(BF16)

        first = diagonal(top[:, :hf], 0)
        last = diagonal(low_scores, hf)
        decay = jnp.exp(run[:, hf:] - runc[:hf])
        weight = decay * lw[depth][:, hf:]
        scores = top[:, hf:]
        corner = weight, scores * decay, (scores * weight).astype(BF16)
        mt = jnp.concatenate(
            [
                jnp.concatenate([first[2], corner[2]], axis=1),
                jnp.concatenate([jnp.zeros((hf, hf), BF16), last[2]], axis=1),
            ],
            axis=0,
        )
        mixed = tn(mt, v)
        qt = q.astype(F32).T
        exp_run = jnp.exp(run)
        scaled = [(qt * (lw[depth + 1 + bit] * exp_run)).astype(BF16) for bit in range(levels)]

        def store():
            for place, part in enumerate((first, corner, last)):
                w_s[h, place] = part[0]
                sd_s[h, place] = part[1]
            mt_s[h] = mt
            mixed_s[h] = mixed
            qt_s[h] = qt
            for bit in range(levels):
                qst_s[h, bit * state : (bit + 1) * state] = scaled[bit]

        return store

    def merge(bit, i):
        h = own_start + i
        mine, theirs = own_s[bit, h], oth_s[bit, h]
        own_rate, other_rate = mine[state : state + 1], theirs[state : state + 1]
        own_f = jnp.where(upper(bit), 1.0, jnp.exp(other_rate))
        other_f = jnp.where(upper(bit), jnp.exp(own_rate), 1.0)
        own_s[bit + 1, h, :state] = own_f * mine[:state] + other_f * theirs[:state]
        own_s[bit + 1, h, state:] = mine[state:] + theirs[state:]

    together(forward, range(group))
    done = group
    state_copy(own_start, 0).wait_recv()
    state_copy(own_start, 1).wait_recv()
    if levels > 1:

        @pl.loop(0, hh)
        def _(i):
            merge(0, i)
            link_copy(1, i, mates[1]).start()

    for bit in range(1, levels - 1):
        if done + group <= heads:
            together(forward, range(done, done + group))
            done += group
        ahead_of = min(heads - done, hh)

        @pl.loop(0, hh // group)
        def _(j, bit=bit, done=done, ahead_of=ahead_of):
            for n in range(group):
                i = group * j + n
                link_copy(bit, i, mates[bit]).wait_recv()
                merge(bit, i)
                link_copy(bit + 1, i, mates[bit + 1]).start()
                pass_copy(bit, own_start + i).start()

            @pl.when(group * j < ahead_of)
            def _():
                together(forward, [done + group * j + n for n in range(group)])

        done += ahead_of

    if done < heads:
        sweep(forward, done, heads - done)

    def outer(h):
        ahead = jnp.zeros((1, state), F32)
        shares, buckets = [], []
        for bit in range(levels):
            taken = jnp.where(upper(bit), jnp.exp(ahead), 0.0)
            shares.append(taken)
            buckets.append((taken * oth_s[bit, h, :state]).astype(BF16))
            ahead = ahead + jnp.where(upper(bit), oth_s[bit, h, state : state + 1], 0.0)
        mixed = mixed_s[h] + tn(qst_s[h], jnp.concatenate(buckets, axis=0))
        z = z_ref[h].astype(F32)
        gated = mixed * (z * jax.nn.sigmoid(z))
        scaled = dy_ref[h].astype(F32) * gain_ref[pl.ds(h, 1), :]

        def store():
            for bit in range(levels):
                taken_s[bit, h] = shares[bit]
                bks_s[h, bit * state : (bit + 1) * state] = buckets[bit]
            mixed_s[h] = mixed
            acc_s[0] += gated * gated
            acc_s[1] += gated * scaled

        return store

    for load in loads[5:]:
        load.wait()

    @pl.loop(0, hh // group)
    def _(j):
        places = [own_start + group * j + n for n in range(group)]
        if levels > 1:
            for n in range(group):
                link_copy(levels - 1, group * j + n, mates[levels - 1]).wait_recv()
                pass_copy(levels - 1, places[n]).start()
        together(outer, places)

    @pl.loop(0, hh // group)
    def _(j):
        places = [other_start + group * j + n for n in range(group)]
        for h in places:
            for bit in range(1, levels):
                pass_copy(bit, h).wait_recv()
        together(outer, places)

    pick = lax.broadcasted_iota(jnp.int32, (8, state), 0)
    sums = nt(jnp.where(pick == 0, 1.0, 0.0), acc_s[0], HIGH) + nt(jnp.where(pick == 1, 1.0, 0.0), acc_s[1], HIGH)
    nsend_s[...] = sums
    for d in range(1, head_count):
        norm_copy(d).start()
    for d in range(1, head_count):
        norm_copy(d).wait_recv()
        sums = sums + nrecv_s[d - 1]
    inverse = lax.rsqrt(sums[0:1] / total + EPSILON)
    pull = inverse * inverse * inverse * sums[1:2] / total
    columns = jnp.where(lax.broadcasted_iota(jnp.int32, (8, width), 0) == 0, inverse, pull).T
    col_s[0] = jnp.broadcast_to(columns[:, 0:1], (width, state))
    col_s[1] = jnp.broadcast_to(columns[:, 1:2], (width, state))

    def gate_back(h):
        z = z_ref[h].astype(F32)
        sig = jax.nn.sigmoid(z)
        act = z * sig
        mixed = mixed_s[h]
        gated = mixed * act
        gain = gain_ref[pl.ds(h, 1), :]
        dy = dy_ref[h].astype(F32)
        inv = col_s[0]
        normed = gated * inv
        shown = (gain * normed).astype(BF16)
        gain_sum = jnp.sum(dy * normed, axis=0, keepdims=True)
        grad = inv * (dy * gain) - gated * col_s[1]
        gz = (grad * mixed * sig * (1.0 + z * (1.0 - sig))).astype(BF16)
        gx = (grad * act).astype(BF16)
        grads = nn(qst_s[h], gx)
        parts = [taken_s[bit, h] * grads[bit * state : (bit + 1) * state] for bit in range(levels)]

        def store():
            lo_ref[h] = shown
            gsend_s[0, pl.ds(h, 1), :] = gain_sum
            gz_ref[h] = gz
            gx_s[h] = gx
            bg_s[h] = parts[0]
            for bit in range(1, levels):
                e_s[h, bit - 1] = parts[bit]

        return store

    sweep(gate_back, other_start, hh)
    if levels > 1:
        e_copy().start()

    sweep(gate_back, own_start, hh)
    bg_copy().start()
    gain_copy(0).start()

    def send_down(bit, i):
        h = own_start + i
        e = e_s[h, bit - 1] + er_s[i, bit - 1]
        if bit < levels - 1:
            rate, other_rate = own_s[bit, h, state : state + 1], oth_s[bit, h, state : state + 1]
            other_f = jnp.where(upper(bit), jnp.exp(rate), 1.0)
            e = e + other_f * d_s[i]
        dmsg_s[bit, i] = e
        d_copy(bit, i, mates[bit]).start()

    def take_down(bit, i):
        h = own_start + i
        d_copy(bit, i, mates[bit]).wait_recv()
        got = dr_s[bit, i]
        if bit < levels - 1:
            other_rate = oth_s[bit, h, state : state + 1]
            own_f = jnp.where(upper(bit), 1.0, jnp.exp(other_rate))
            got = got + own_f * d_s[i]
        if bit > 1:
            d_s[i] = got
        else:
            dfull_s[h] = got

    if levels > 1:
        e_copy().wait_recv()

        @pl.loop(0, hh)
        def _(i):
            send_down(levels - 1, i)
    else:
        dfull_s[...] = jnp.zeros_like(dfull_s)

    def block_grads(h):
        q, k, v, gx = q_ref[h], k_ref[h], v_ref[h], gx_s[h]
        lev = lev_s[...]
        top = nt(v[:hf], gx)
        low_grads = nt(v[hf:], gx[hf:])
        parts = ((top[:, :hf], 0), (top[:, hf:], hf), (low_grads, hf))
        spread = [(part * w_s[h, place]).astype(BF16) for place, (part, lo) in enumerate(parts)]
        gst = jnp.concatenate(
            [
                jnp.concatenate([spread[0], spread[1]], axis=1),
                jnp.concatenate([jnp.zeros((hf, hf), BF16), spread[2]], axis=1),
            ],
            axis=0,
        )
        moved = [parts[place][0] * sd_s[h, place] for place in (0, 2)]
        rows = [
            jnp.concatenate(
                [jnp.sum(jnp.where(lev == step, part, 0.0), axis=0, keepdims=True) for part in moved], axis=1
            )
            for step in range(depth)
        ]
        corner = jnp.sum(top[:, hf:] * sd_s[h, 1], axis=0, keepdims=True)
        rows.append(jnp.concatenate([jnp.zeros((1, hf), F32), corner], axis=1))
        gkin = nn(gst, q)
        gvin = nn(mt_s[h], gx)
        gqt = tn(k, gst)
        pulled = nt(bks_s[h], gx)
        exp_run = jnp.exp(run_s[h])
        qt = qt_s[h]
        outs = []
        for bit in range(levels):
            here = pulled[bit * state : (bit + 1) * state]
            outs.append(exp_run * jnp.sum(qt * here, axis=0, keepdims=True))
            gqt = gqt + (lw_ref[depth + 1 + bit, pl.ds(h, 1), :] * exp_run) * here
        gq = gqt.T.astype(BF16)

        def store():
            here = lax.broadcasted_iota(jnp.int32, (heads, width), 0) == h
            for step, line in enumerate(rows + outs):
                gl_ref[step] = jnp.where(here, line, gl_ref[step])
            gkin_s[h] = gkin
            gvin_s[h] = gvin
            gq_ref[h] = gq

        return store

    gl_ref[...] = jnp.zeros_like(gl_ref)
    done = 0
    for bit in range(levels - 1, 0, -1):
        if done + group <= heads:
            together(block_grads, range(done, done + group))
            done += group
        ahead_of = min(heads - done, hh)
        turn = levels - 1 - bit
        gain_copy(turn).wait_recv()
        gsend_s[turn + 1] = gsend_s[turn] + grecv_s[turn]
        gain_copy(turn + 1).start()

        @pl.loop(0, hh // group)
        def _(j, bit=bit, done=done, ahead_of=ahead_of):
            for n in range(group):
                i = group * j + n
                take_down(bit, i)
                if bit > 1:
                    send_down(bit - 1, i)
                else:
                    half_copy(own_start + i).start()

            @pl.when(group * j < ahead_of)
            def _():
                together(block_grads, [done + group * j + n for n in range(group)])

        done += ahead_of

    if done < heads:
        sweep(block_grads, done, heads - done)

    gain_copy(levels - 1).wait_recv()
    gg_ref[...] = gsend_s[levels - 1] + grecv_s[levels - 1]
    bg_copy().wait_recv()

    def finish(h):
        own_f = jnp.where(upper(0), 1.0, jnp.exp(oth_s[0, h, state : state + 1]))
        down = (own_f * dfull_s[h] + bgr_s[h]).astype(BF16)
        tail = tailc_s[h]
        gk = (gkin_s[h] + tail * nt(v_ref[h], down)).astype(BF16)
        gv = (gvin_s[h] + tail * nn(k_ref[h], down)).astype(BF16)

        def store():
            gk_ref[h] = gk
            gv_ref[h] = gv

        return store

    sweep(finish, own_start, hh)
    if levels > 1:

        @pl.loop(0, hh)
        def _(i):
            half_copy(other_start + i).wait_recv()

    sweep(finish, other_start, hh)

    state_copy(other_start, 0).wait_send()
    state_copy(own_start, 1).wait_send()
    bg_copy().wait_send()
    for d in range(1, head_count):
        norm_copy(d).wait_send()
    for bit in range(levels):
        gain_copy(bit).wait_send()
    if levels > 1:
        e_copy().wait_send()

        @pl.loop(0, hh)
        def _(i):
            half_copy(own_start + i).wait_send()
            for bit in range(1, levels):
                link_copy(bit, i, mates[bit]).wait_send()
                pass_copy(bit, own_start + i).wait_send()
                d_copy(bit, i, mates[bit]).wait_send()


def copy_kernel(*refs):
    count = len(refs) // 2
    sems = refs[-1]
    copies = [pltpu.make_async_copy(refs[at], refs[count + at], sems.at[at]) for at in range(count)]
    for copy in copies:
        copy.start()
    for copy in copies:
        copy.wait()


def local(levels, head_count, queries, keys, values, log_decay, level_weight, gate_input, norm_gain, out_grad):
    heads, width, state = queries.shape
    feature = values.shape[2]
    hf, hh = width // 2, heads // 2
    total = heads * head_count * feature
    tokens = jax.ShapeDtypeStruct(queries.shape, BF16)
    vmem = pl.BlockSpec(memory_space=pltpu.VMEM)

    def f32(*shape):
        return pltpu.VMEM(shape, F32)

    def bf16(*shape):
        return pltpu.VMEM(shape, BF16)

    dma = pltpu.SemaphoreType.DMA
    more = max(levels - 1, 1)
    scratch = [
        bf16(heads, width, state), bf16(heads, width, feature),
        f32(heads, width, state), f32(heads, width, feature), f32(heads, width, feature),
        bf16(heads, width, state), f32(heads, width), f32(level_weight.shape[1], heads, width),
        bf16(heads, width, feature), f32(heads, feature), bf16(heads, width, feature),
        f32(heads, 1, width), f32(heads, 1, width), f32(heads, width, hf),
        pltpu.VMEM((hf, hf), jnp.int32),
        f32(levels, heads, state + PAD, feature), f32(levels, heads, state + PAD, feature),
        f32(heads, 3, hf, hf), f32(heads, 3, hf, hf), bf16(heads, width, width),
        bf16(heads, levels * state, width), f32(heads, state, width),
        f32(heads, width, feature), bf16(heads, levels * state, feature), f32(levels, heads, 1, feature),
        f32(2, width, feature), f32(8, width), f32(max(head_count - 1, 1), 8, width),
        f32(2, width, feature), bf16(heads, width, feature),
        f32(heads, more, state, feature), f32(hh, more, state, feature),
        f32(heads, state, feature), f32(heads, state, feature),
        f32(levels, hh, state, feature), f32(levels, hh, state, feature), f32(hh, state, feature),
        f32(heads, state, feature),
        f32(levels, heads, feature), f32(levels, heads, feature),
        dma((8,)),
        dma((levels, heads)), dma((levels, heads)), dma((levels, heads)),
        dma((max(head_count - 1, 1),)), dma((max(head_count - 1, 1),)), dma, dma, dma, dma,
        dma((levels, hh)), dma((levels, hh)), dma((heads,)), dma((heads,)), dma((levels,)), dma((levels,)),
    ]
    hbm = pl.BlockSpec(memory_space=pltpu.HBM)
    turned = jax.ShapeDtypeStruct((level_weight.shape[1], heads, width), F32)
    gains = jax.ShapeDtypeStruct(norm_gain.shape, F32)
    shapes = (tokens, tokens, tokens, tokens, turned, tokens, gains)
    outs = pl.pallas_call(
        functools.partial(kernel, levels, head_count, total),
        out_shape=shapes,
        in_specs=[hbm] * 8,
        out_specs=(vmem,) * 7,
        scratch_shapes=scratch,
        compiler_params=pltpu.CompilerParams(
            collective_id=0, has_side_effects=True, vmem_limit_bytes=51 * 1024 * 1024
        ),
    )(
        queries, keys, values, log_decay, jnp.transpose(level_weight, (1, 0, 2)), gate_input, norm_gain, out_grad
    )
    lo, gq, gk, gv, gl, gz, gg = pl.pallas_call(
        copy_kernel,
        out_shape=shapes,
        in_specs=[pl.BlockSpec(memory_space=pl.ANY)] * 7,
        out_specs=(hbm,) * 7,
        scratch_shapes=[dma((7,))],
    )(*outs)
    return lo, gq, gk, gv, jnp.transpose(gl, (1, 0, 2)), gz, gg


def solution(mesh):
    levels = mesh.shape["seq"].bit_length() - 1
    tokens = P("head", "seq", None)
    in_specs = (tokens, tokens, tokens, P("head", "seq"), P("head", None, "seq"), tokens, P("head", None), tokens)
    out_specs = (tokens, tokens, tokens, tokens, P("head", None, "seq"), tokens, P("head", None))
    return jax.shard_map(
        functools.partial(local, levels, mesh.shape["head"]),
        mesh=mesh, in_specs=in_specs, out_specs=out_specs, check_vma=False,
    )
```

time: 55.7 us -> 136 us (2.44)
  Pallas kernels: 43.1 us -> 127 us
  local copies, waits for them, and re-layouts: 11.5 us -> 7.51 us
    pallas_call x0 -> x1, Pallas kernels: none -> 85.9 us  [local(): pl.pallas_call(copy_kernel, out_shape=shapes, in_specs=[pl.BlockSpec(memo...]
    unnamed x21 -> x20, local copies, waits for them, and re-layouts: 10.8 us -> 7.51 us
    pallas_call x1, Pallas kernels: 43.1 us -> 41.4 us  [local(): pl.pallas_call(functools.partial(kernel, levels, head_count, total), out_...]
where the time goes in v2:
time: 136 us; the launch traced here: 135 us
  Pallas kernels  127 us (93%)
  local copies, waits for them, and re-layouts  7.51 us (6%)
    pallas_call x1, Pallas kernels, local(): pl.pallas_call(copy_kernel, out_shape=shapes, in_specs=[pl.BlockSpec(memo...  85.9 us
    pallas_call x1, Pallas kernels, local(): pl.pallas_call(functools.partial(kernel, levels, head_count, total), out_...  41.4 us
    unnamed x20, local copies, waits for them, and re-layouts  7.51 us

profile of v2, /device:TPU:0, one launch (start us, length us, event | category | flops | bytes accessed | tf_op | source)
XLA Modules:
  0.0 135.5 jit_solution(6047903226659830935)
XLA Ops:
  0.6 0.0 copy-start.5
  0.6 0.9 copy-done.5
  1.6 0.0 copy-start.7
  1.6 0.7 copy-done.7
  2.3 0.0 copy-start.8
  2.3 0.7 copy-done.8
  2.9 41.4 %shard_map.135 = (bf16[8,256,128]{2,1,0:T(8,128)(2,1)S(1)}, bf16[8,256,128]{2,1,0:T(8,128)(2,1)S(1)}, bf16[8,256,128]{2,1,0:T(8,128)(2,1)S(1)}, bf16[8,256,128]{...) custom-call(bf16[8,256,128]{2,1,0:T(8,128)(2,1)} %q_in.1, ...), custom_call_target="tpu_custom_call" | custom-call | tf_op jit(solution)/shard_map/pallas_call | solution.py:561
  44.3 0.0 copy-start
  44.4 0.8 copy-done
  45.1 0.0 copy-start.1
  45.1 0.8 copy-done.1
  45.9 0.0 copy-start.2
  45.9 0.8 copy-done.2
  46.7 0.0 copy-start.3
  46.7 0.8 copy-done.3
  47.5 0.0 copy-start.4
  47.5 0.8 copy-done.4
  48.3 0.0 copy-start.6
  48.3 0.7 copy-done.6
  49.0 0.0 copy-start.9
  49.0 0.6 copy-done.9
  49.6 85.9 %shard_map.136 = (bf16[8,256,128]{2,1,0:T(8,128)(2,1)}, bf16[8,256,128]{2,1,0:T(8,128)(2,1)}, bf16[8,256,128]{2,1,0:T(8,128)(2,1)}, bf16[8,256,128]{2,1,0:T(8,12...) custom-call(bf16[8,256,128]{2,1,0:T(8,128)(2,1)} %copy-done, ...), custom_call_target="tpu_custom_call" | custom-call | tf_op jit(solution)/shard_map/pallas_call | solution.py:573
Async XLA Ops:
  0.6 0.9 copy-start.5
  1.6 0.7 copy-start.7
  2.3 0.7 copy-start.8
  44.3 0.8 copy-start
  45.1 0.8 copy-start.1
  45.9 0.8 copy-start.2
  46.7 0.8 copy-start.3
  47.5 0.8 copy-start.4
  48.3 0.7 copy-start.6
  49.0 0.6 copy-start.9

commit v3 on v2

--- a/solution.py
+++ b/solution.py
@@ -347,10 +347,6 @@
     if levels > 1:
         e_copy().start()
 
-    sweep(gate_back, own_start, hh)
-    bg_copy().start()
-    gain_copy(0).start()
-
     def send_down(bit, i):
         h = own_start + i
         e = e_s[h, bit - 1] + er_s[i, bit - 1]
@@ -374,13 +370,21 @@
         else:
             dfull_s[h] = got
 
-    if levels > 1:
-        e_copy().wait_recv()
-
-        @pl.loop(0, hh)
-        def _(i):
-            send_down(levels - 1, i)
-    else:
+    @pl.loop(0, hh // group)
+    def _(j):
+        together(gate_back, [own_start + group * j + n for n in range(group)])
+        if levels > 1:
+
+            @pl.when(j == 0)
+            def _():
+                e_copy().wait_recv()
+
+            for n in range(group):
+                send_down(levels - 1, group * j + n)
+
+    bg_copy().start()
+    gain_copy(0).start()
+    if levels == 1:
         dfull_s[...] = jnp.zeros_like(dfull_s)
 
     def block_grads(h):
@@ -429,9 +433,22 @@
 
         return store
 
+    def finish(h):
+        own_f = jnp.where(upper(0), 1.0, jnp.exp(oth_s[0, h, state : state + 1]))
+        down = (own_f * dfull_s[h] + bgr_s[h]).astype(BF16)
+        tail = tailc_s[h]
+        gk = (gkin_s[h] + tail * nt(v_ref[h], down)).astype(BF16)
+        gv = (gvin_s[h] + tail * nn(k_ref[h], down)).astype(BF16)
+
+        def store():
+            gk_ref[h] = gk
+            gv_ref[h] = gv
+
+        return store
+
     gl_ref[...] = jnp.zeros_like(gl_ref)
     done = 0
-    for bit in range(levels - 1, 0, -1):
+    for bit in range(levels - 1, 1, -1):
         if done + group <= heads:
             together(block_grads, range(done, done + group))
             done += group
@@ -446,10 +463,7 @@
             for n in range(group):
                 i = group * j + n
                 take_down(bit, i)
-                if bit > 1:
-                    send_down(bit - 1, i)
-                else:
-                    half_copy(own_start + i).start()
+                send_down(bit - 1, i)
 
             @pl.when(group * j < ahead_of)
             def _():
@@ -459,33 +473,32 @@
 
     if done < heads:
         sweep(block_grads, done, heads - done)
+    if levels > 1:
+        turn = levels - 2
+        gain_copy(turn).wait_recv()
+        gsend_s[turn + 1] = gsend_s[turn] + grecv_s[turn]
+        gain_copy(turn + 1).start()
+    bg_copy().wait_recv()
+
+    @pl.loop(0, hh // group)
+    def _(j):
+        places = [group * j + n for n in range(group)]
+        if levels > 1:
+            for i in places:
+                take_down(1, i)
+                half_copy(own_start + i).start()
+        together(finish, [own_start + i for i in places])
+
+    @pl.loop(0, hh // group)
+    def _(j):
+        places = [other_start + group * j + n for n in range(group)]
+        if levels > 1:
+            for h in places:
+                half_copy(h).wait_recv()
+        together(finish, places)
 
     gain_copy(levels - 1).wait_recv()
     gg_ref[...] = gsend_s[levels - 1] + grecv_s[levels - 1]
-    bg_copy().wait_recv()
-
-    def finish(h):
-        own_f = jnp.where(upper(0), 1.0, jnp.exp(oth_s[0, h, state : state + 1]))
-        down = (own_f * dfull_s[h] + bgr_s[h]).astype(BF16)
-        tail = tailc_s[h]
-        gk = (gkin_s[h] + tail * nt(v_ref[h], down)).astype(BF16)
-        gv = (gvin_s[h] + tail * nn(k_ref[h], down)).astype(BF16)
-
-        def store():
-            gk_ref[h] = gk
-            gv_ref[h] = gv
-
-        return store
-
-    sweep(finish, own_start, hh)
-    if levels > 1:
-
-        @pl.loop(0, hh)
-        def _(i):
-            half_copy(other_start + i).wait_recv()
-
-    sweep(finish, other_start, hh)
-
     state_copy(other_start, 0).wait_send()
     state_copy(own_start, 1).wait_send()
     bg_copy().wait_send()
@@ -565,7 +578,7 @@
         out_specs=(vmem,) * 7,
         scratch_shapes=scratch,
         compiler_params=pltpu.CompilerParams(
-            collective_id=0, has_side_effects=True, vmem_limit_bytes=51 * 1024 * 1024
+            collective_id=0, has_side_effects=True, vmem_limit_bytes=52224 * 1024
         ),
     )(
         queries, keys, values, log_decay, jnp.transpose(level_weight, (1, 0, 2)), gate_input, norm_gain, out_grad
@@ -573,7 +586,7 @@
     lo, gq, gk, gv, gl, gz, gg = pl.pallas_call(
         copy_kernel,
         out_shape=shapes,
-        in_specs=[pl.BlockSpec(memory_space=pl.ANY)] * 7,
+        in_specs=[vmem] * 7,
         out_specs=(hbm,) * 7,
         scratch_shapes=[dma((7,))],
     )(*outs)

time: 136 us -> 52.1 us (0.38)
  Pallas kernels: 127 us -> 43.7 us
    pallas_call x1, Pallas kernels: 85.9 us -> 3.31 us  [local(): pl.pallas_call(copy_kernel, out_shape=shapes, in_specs=[vmem] * 7, out_sp...]
where the time goes in v3:
time: 52.1 us; the launch traced here: 51.9 us
  Pallas kernels  43.7 us (84%)
  local copies, waits for them, and re-layouts  7.51 us (14%)
  between operations  0.67 us (1%)
    pallas_call x1, Pallas kernels, local(): pl.pallas_call(functools.partial(kernel, levels, head_count, total), out_...  40.4 us
    unnamed x20, local copies, waits for them, and re-layouts  7.51 us
    pallas_call x1, Pallas kernels, local(): pl.pallas_call(copy_kernel, out_shape=shapes, in_specs=[vmem] * 7, out_sp...  3.31 us

profile of v3, /device:TPU:0, one launch (start us, length us, event | category | flops | bytes accessed | tf_op | source)
XLA Modules:
  0.0 51.9 jit_solution(2598621512275456909)
XLA Ops:
  0.6 0.0 copy-start.5
  0.6 0.9 %copy-done.5 = f32[8,21,256]{2,0,1:T(8,128)S(1)} copy-done((f32[8,21,256]{2,0,1:T(8,128)S(1)}, f32[8,21,256]{2,0,1:T(8,128)}, u32[]{:S(2)}) %copy-start.5) | copy-done | bytes 172056
  1.6 0.0 copy-start.7
  1.6 0.7 %copy-done.7 = f32[8,256]{1,0:T(8,128)S(1)} copy-done((f32[8,256]{1,0:T(8,128)S(1)}, f32[8,256]{1,0:T(8,128)}, u32[]{:S(2)}) %copy-start.7) | copy-done | bytes 8216
  2.3 0.0 copy-start.8
  2.3 0.7 %copy-done.8 = f32[8,128]{1,0:T(8,128)S(1)} copy-done((f32[8,128]{1,0:T(8,128)S(1)}, f32[8,128]{1,0:T(8,128)}, u32[]{:S(2)}) %copy-start.8) | copy-done | bytes 4120
  2.9 40.4 %shard_map.135 = (bf16[8,256,128]{2,1,0:T(8,128)(2,1)S(1)}, bf16[8,256,128]{2,1,0:T(8,128)(2,1)S(1)}, bf16[8,256,128]{2,1,0:T(8,128)(2,1)S(1)}, bf16[8,256,128]{...) custom-call(bf16[8,256,128]{2,1,0:T(8,128)(2,1)} %q_in.1, ...), custom_call_target="tpu_custom_call" | custom-call | tf_op jit(solution)/shard_map/pallas_call | solution.py:574
  43.3 0.0 copy-start
  43.4 0.8 %copy-done = bf16[8,256,128]{2,1,0:T(8,128)(2,1)} copy-done((bf16[8,256,128]{2,1,0:T(8,128)(2,1)}, bf16[8,256,128]{2,1,0:T(8,128)(2,1)S(1)}, u32[]{:S(2)}) %copy-start) | copy-done | bytes 524312
  44.1 0.0 copy-start.1
  44.1 0.8 %copy-done.1 = bf16[8,256,128]{2,1,0:T(8,128)(2,1)} copy-done((bf16[8,256,128]{2,1,0:T(8,128)(2,1)}, bf16[8,256,128]{2,1,0:T(8,128)(2,1)S(1)}, u32[]{:S(2)}) %copy-start.1) | copy-done | bytes 524312
  44.9 0.0 copy-start.2
  44.9 0.8 %copy-done.2 = bf16[8,256,128]{2,1,0:T(8,128)(2,1)} copy-done((bf16[8,256,128]{2,1,0:T(8,128)(2,1)}, bf16[8,256,128]{2,1,0:T(8,128)(2,1)S(1)}, u32[]{:S(2)}) %copy-start.2) | copy-done | bytes 524312
  45.7 0.0 copy-start.3
  45.7 0.8 %copy-done.3 = bf16[8,256,128]{2,1,0:T(8,128)(2,1)} copy-done((bf16[8,256,128]{2,1,0:T(8,128)(2,1)}, bf16[8,256,128]{2,1,0:T(8,128)(2,1)S(1)}, u32[]{:S(2)}) %copy-start.3) | copy-done | bytes 524312
  46.5 0.0 copy-start.4
  46.5 0.8 %copy-done.4 = bf16[8,256,128]{2,1,0:T(8,128)(2,1)} copy-done((bf16[8,256,128]{2,1,0:T(8,128)(2,1)}, bf16[8,256,128]{2,1,0:T(8,128)(2,1)S(1)}, u32[]{:S(2)}) %copy-start.4) | copy-done | bytes 524312
  47.3 0.0 copy-start.6
  47.3 0.7 %copy-done.6 = f32[21,8,256]{2,1,0:T(8,128)} copy-done((f32[21,8,256]{2,1,0:T(8,128)}, f32[21,8,256]{2,1,0:T(8,128)S(1)}, u32[]{:S(2)}) %copy-start.6) | copy-done | bytes 172056
  48.0 0.0 copy-start.9
  48.0 0.6 %copy-done.9 = f32[8,128]{1,0:T(8,128)} copy-done((f32[8,128]{1,0:T(8,128)}, f32[8,128]{1,0:T(8,128)S(1)}, u32[]{:S(2)}) %copy-start.9) | copy-done | bytes 4120
  48.6 3.3 %shard_map.136 = (bf16[8,256,128]{2,1,0:T(8,128)(2,1)}, bf16[8,256,128]{2,1,0:T(8,128)(2,1)}, bf16[8,256,128]{2,1,0:T(8,128)(2,1)}, bf16[8,256,128]{2,1,0:T(8,12...) custom-call(bf16[8,256,128]{2,1,0:T(8,128)(2,1)} %copy-done, ...), custom_call_target="tpu_custom_call" | custom-call | tf_op jit(solution)/shard_map/pallas_call | solution.py:586
Async XLA Ops:
  0.6 0.9 %copy-start.5 = (f32[8,21,256]{2,0,1:T(8,128)S(1)}, f32[8,21,256]{2,0,1:T(8,128)}, u32[]{:S(2)}) copy-start(f32[8,21,256]{2,0,1:T(8,128)} %param.12) | copy-start | bytes 516100
  1.6 0.7 %copy-start.7 = (f32[8,256]{1,0:T(8,128)S(1)}, f32[8,256]{1,0:T(8,128)}, u32[]{:S(2)}) copy-start(f32[8,256]{1,0:T(8,128)} %ld_in.1) | copy-start | bytes 24580
  2.3 0.7 %copy-start.8 = (f32[8,128]{1,0:T(8,128)S(1)}, f32[8,128]{1,0:T(8,128)}, u32[]{:S(2)}) copy-start(f32[8,128]{1,0:T(8,128)} %gain_in.1) | copy-start | bytes 12292
  43.3 0.8 %copy-start = (bf16[8,256,128]{2,1,0:T(8,128)(2,1)}, bf16[8,256,128]{2,1,0:T(8,128)(2,1)S(1)}, u32[]{:S(2)}) copy-start(bf16[8,256,128]{2,1,0:T(8,128)(2,1)S(1)} %get-tuple-element.21.refs_0_) | copy-start | bytes 1572868
  44.1 0.8 %copy-start.1 = (bf16[8,256,128]{2,1,0:T(8,128)(2,1)}, bf16[8,256,128]{2,1,0:T(8,128)(2,1)S(1)}, u32[]{:S(2)}) copy-start(bf16[8,256,128]{2,1,0:T(8,128)(2,1)S(1)} %get-tuple-element.22.refs_1_) | copy-start | bytes 1572868
  44.9 0.8 %copy-start.2 = (bf16[8,256,128]{2,1,0:T(8,128)(2,1)}, bf16[8,256,128]{2,1,0:T(8,128)(2,1)S(1)}, u32[]{:S(2)}) copy-start(bf16[8,256,128]{2,1,0:T(8,128)(2,1)S(1)} %get-tuple-element.23.refs_2_) | copy-start | bytes 1572868
  45.7 0.8 %copy-start.3 = (bf16[8,256,128]{2,1,0:T(8,128)(2,1)}, bf16[8,256,128]{2,1,0:T(8,128)(2,1)S(1)}, u32[]{:S(2)}) copy-start(bf16[8,256,128]{2,1,0:T(8,128)(2,1)S(1)} %get-tuple-element.24.refs_3_) | copy-start | bytes 1572868
  46.5 0.8 %copy-start.4 = (bf16[8,256,128]{2,1,0:T(8,128)(2,1)}, bf16[8,256,128]{2,1,0:T(8,128)(2,1)S(1)}, u32[]{:S(2)}) copy-start(bf16[8,256,128]{2,1,0:T(8,128)(2,1)S(1)} %get-tuple-element.26.refs_5_) | copy-start | bytes 1572868
  47.3 0.7 %copy-start.6 = (f32[21,8,256]{2,1,0:T(8,128)}, f32[21,8,256]{2,1,0:T(8,128)S(1)}, u32[]{:S(2)}) copy-start(f32[21,8,256]{2,1,0:T(8,128)S(1)} %get-tuple-element.25.refs_4_) | copy-start | bytes 516100
  48.0 0.6 %copy-start.9 = (f32[8,128]{1,0:T(8,128)}, f32[8,128]{1,0:T(8,128)S(1)}, u32[]{:S(2)}) copy-start(f32[8,128]{1,0:T(8,128)S(1)} %get-tuple-element.27.refs_6_) | copy-start | bytes 12292

commit v4 on v3

--- a/solution.py
+++ b/solution.py
@@ -578,7 +578,7 @@
         out_specs=(vmem,) * 7,
         scratch_shapes=scratch,
         compiler_params=pltpu.CompilerParams(
-            collective_id=0, has_side_effects=True, vmem_limit_bytes=52224 * 1024
+            collective_id=0, has_side_effects=True, vmem_limit_bytes=51680 * 1024
         ),
     )(
         queries, keys, values, log_decay, jnp.transpose(level_weight, (1, 0, 2)), gate_input, norm_gain, out_grad

time: 52.1 us -> 53.3 us (1.023)
  local copies, waits for them, and re-layouts: 7.51 us -> 8.6 us
    unnamed x20 -> x22, local copies, waits for them, and re-layouts: 7.51 us -> 8.6 us
where the time goes in v4:
time: 53.3 us; the launch traced here: 53 us
  Pallas kernels  43.7 us (82%)
  local copies, waits for them, and re-layouts  8.6 us (16%)
  between operations  0.67 us (1%)
    pallas_call x1, Pallas kernels, local(): pl.pallas_call(functools.partial(kernel, levels, head_count, total), out_...  40.4 us
    unnamed x22, local copies, waits for them, and re-layouts  8.6 us
    pallas_call x1, Pallas kernels, local(): pl.pallas_call(copy_kernel, out_shape=shapes, in_specs=[vmem] * 7, out_sp...  3.31 us

profile of v4, /device:TPU:0, one launch (start us, length us, event | category | flops | bytes accessed | tf_op | source)
XLA Modules:
  0.0 53.0 jit_solution(8956684810683421526)
XLA Ops:
  0.6 0.0 copy-start
  0.6 1.0 %copy-done = bf16[8,256,128]{2,1,0:T(8,128)(2,1)S(1)} copy-done((bf16[8,256,128]{2,1,0:T(8,128)(2,1)S(1)}, bf16[8,256,128]{2,1,0:T(8,128)(2,1)}, u32[]{:S(2)}) %copy-start) | copy-done | bytes 524312
  1.7 0.0 copy-start.6
  1.7 0.9 %copy-done.6 = f32[8,21,256]{2,0,1:T(8,128)S(1)} copy-done((f32[8,21,256]{2,0,1:T(8,128)S(1)}, f32[8,21,256]{2,0,1:T(8,128)}, u32[]{:S(2)}) %copy-start.6) | copy-done | bytes 172056
  2.6 0.0 copy-start.8
  2.6 0.7 %copy-done.8 = f32[8,256]{1,0:T(8,128)S(1)} copy-done((f32[8,256]{1,0:T(8,128)S(1)}, f32[8,256]{1,0:T(8,128)}, u32[]{:S(2)}) %copy-start.8) | copy-done | bytes 8216
  3.3 0.0 copy-start.9
  3.3 0.7 %copy-done.9 = f32[8,128]{1,0:T(8,128)S(1)} copy-done((f32[8,128]{1,0:T(8,128)S(1)}, f32[8,128]{1,0:T(8,128)}, u32[]{:S(2)}) %copy-start.9) | copy-done | bytes 4120
  4.0 40.4 %shard_map.135 = (bf16[8,256,128]{2,1,0:T(8,128)(2,1)S(1)}, bf16[8,256,128]{2,1,0:T(8,128)(2,1)S(1)}, bf16[8,256,128]{2,1,0:T(8,128)(2,1)S(1)}, bf16[8,256,128]{...) custom-call(bf16[8,256,128]{2,1,0:T(8,128)(2,1)S(1)} %copy-done, ...), custom_call_target="tpu_custom_call" | custom-call | tf_op jit(solution)/shard_map/pallas_call | solution.py:574
  44.4 0.0 copy-start.1
  44.4 0.8 %copy-done.1 = bf16[8,256,128]{2,1,0:T(8,128)(2,1)} copy-done((bf16[8,256,128]{2,1,0:T(8,128)(2,1)}, bf16[8,256,128]{2,1,0:T(8,128)(2,1)S(1)}, u32[]{:S(2)}) %copy-start.1) | copy-done | bytes 524312
  45.2 0.0 copy-start.2
  45.2 0.8 %copy-done.2 = bf16[8,256,128]{2,1,0:T(8,128)(2,1)} copy-done((bf16[8,256,128]{2,1,0:T(8,128)(2,1)}, bf16[8,256,128]{2,1,0:T(8,128)(2,1)S(1)}, u32[]{:S(2)}) %copy-start.2) | copy-done | bytes 524312
  46.0 0.0 copy-start.3
  46.0 0.8 %copy-done.3 = bf16[8,256,128]{2,1,0:T(8,128)(2,1)} copy-done((bf16[8,256,128]{2,1,0:T(8,128)(2,1)}, bf16[8,256,128]{2,1,0:T(8,128)(2,1)S(1)}, u32[]{:S(2)}) %copy-start.3) | copy-done | bytes 524312
  46.8 0.0 copy-start.4
  46.8 0.8 %copy-done.4 = bf16[8,256,128]{2,1,0:T(8,128)(2,1)} copy-done((bf16[8,256,128]{2,1,0:T(8,128)(2,1)}, bf16[8,256,128]{2,1,0:T(8,128)(2,1)S(1)}, u32[]{:S(2)}) %copy-start.4) | copy-done | bytes 524312
  47.7 0.0 copy-start.5
  47.7 0.8 %copy-done.5 = bf16[8,256,128]{2,1,0:T(8,128)(2,1)} copy-done((bf16[8,256,128]{2,1,0:T(8,128)(2,1)}, bf16[8,256,128]{2,1,0:T(8,128)(2,1)S(1)}, u32[]{:S(2)}) %copy-start.5) | copy-done | bytes 524312
  48.5 0.0 copy-start.7
  48.5 0.7 %copy-done.7 = f32[21,8,256]{2,1,0:T(8,128)} copy-done((f32[21,8,256]{2,1,0:T(8,128)}, f32[21,8,256]{2,1,0:T(8,128)S(1)}, u32[]{:S(2)}) %copy-start.7) | copy-done | bytes 172056
  49.1 0.0 copy-start.10
  49.1 0.6 %copy-done.10 = f32[8,128]{1,0:T(8,128)} copy-done((f32[8,128]{1,0:T(8,128)}, f32[8,128]{1,0:T(8,128)S(1)}, u32[]{:S(2)}) %copy-start.10) | copy-done | bytes 4120
  49.7 3.3 %shard_map.136 = (bf16[8,256,128]{2,1,0:T(8,128)(2,1)}, bf16[8,256,128]{2,1,0:T(8,128)(2,1)}, bf16[8,256,128]{2,1,0:T(8,128)(2,1)}, bf16[8,256,128]{2,1,0:T(8,12...) custom-call(bf16[8,256,128]{2,1,0:T(8,128)(2,1)} %copy-done.1, ...), custom_call_target="tpu_custom_call" | custom-call | tf_op jit(solution)/shard_map/pallas_call | solution.py:586
Async XLA Ops:
  0.6 1.0 %copy-start = (bf16[8,256,128]{2,1,0:T(8,128)(2,1)S(1)}, bf16[8,256,128]{2,1,0:T(8,128)(2,1)}, u32[]{:S(2)}) copy-start(bf16[8,256,128]{2,1,0:T(8,128)(2,1)} %q_in.1) | copy-start | bytes 1572868
  1.7 0.9 %copy-start.6 = (f32[8,21,256]{2,0,1:T(8,128)S(1)}, f32[8,21,256]{2,0,1:T(8,128)}, u32[]{:S(2)}) copy-start(f32[8,21,256]{2,0,1:T(8,128)} %param.12) | copy-start | bytes 516100
  2.6 0.7 %copy-start.8 = (f32[8,256]{1,0:T(8,128)S(1)}, f32[8,256]{1,0:T(8,128)}, u32[]{:S(2)}) copy-start(f32[8,256]{1,0:T(8,128)} %ld_in.1) | copy-start | bytes 24580
  3.3 0.7 %copy-start.9 = (f32[8,128]{1,0:T(8,128)S(1)}, f32[8,128]{1,0:T(8,128)}, u32[]{:S(2)}) copy-start(f32[8,128]{1,0:T(8,128)} %gain_in.1) | copy-start | bytes 12292
  44.4 0.8 %copy-start.1 = (bf16[8,256,128]{2,1,0:T(8,128)(2,1)}, bf16[8,256,128]{2,1,0:T(8,128)(2,1)S(1)}, u32[]{:S(2)}) copy-start(bf16[8,256,128]{2,1,0:T(8,128)(2,1)S(1)} %get-tuple-element.21.refs_0_) | copy-start | bytes 1572868
  45.2 0.8 %copy-start.2 = (bf16[8,256,128]{2,1,0:T(8,128)(2,1)}, bf16[8,256,128]{2,1,0:T(8,128)(2,1)S(1)}, u32[]{:S(2)}) copy-start(bf16[8,256,128]{2,1,0:T(8,128)(2,1)S(1)} %get-tuple-element.22.refs_1_) | copy-start | bytes 1572868
  46.0 0.8 %copy-start.3 = (bf16[8,256,128]{2,1,0:T(8,128)(2,1)}, bf16[8,256,128]{2,1,0:T(8,128)(2,1)S(1)}, u32[]{:S(2)}) copy-start(bf16[8,256,128]{2,1,0:T(8,128)(2,1)S(1)} %get-tuple-element.23.refs_2_) | copy-start | bytes 1572868
  46.8 0.8 %copy-start.4 = (bf16[8,256,128]{2,1,0:T(8,128)(2,1)}, bf16[8,256,128]{2,1,0:T(8,128)(2,1)S(1)}, u32[]{:S(2)}) copy-start(bf16[8,256,128]{2,1,0:T(8,128)(2,1)S(1)} %get-tuple-element.24.refs_3_) | copy-start | bytes 1572868
  47.7 0.8 %copy-start.5 = (bf16[8,256,128]{2,1,0:T(8,128)(2,1)}, bf16[8,256,128]{2,1,0:T(8,128)(2,1)S(1)}, u32[]{:S(2)}) copy-start(bf16[8,256,128]{2,1,0:T(8,128)(2,1)S(1)} %get-tuple-element.26.refs_5_) | copy-start | bytes 1572868
  48.5 0.7 %copy-start.7 = (f32[21,8,256]{2,1,0:T(8,128)}, f32[21,8,256]{2,1,0:T(8,128)S(1)}, u32[]{:S(2)}) copy-start(f32[21,8,256]{2,1,0:T(8,128)S(1)} %get-tuple-element.25.refs_4_) | copy-start | bytes 516100
  49.1 0.6 %copy-start.10 = (f32[8,128]{1,0:T(8,128)}, f32[8,128]{1,0:T(8,128)S(1)}, u32[]{:S(2)}) copy-start(f32[8,128]{1,0:T(8,128)S(1)} %get-tuple-element.27.refs_6_) | copy-start | bytes 12292
